TPU v7x, 32 devices: a whole 2x2x4 slice. The times are simulated.
32 devices in a mesh: det: 8 (over z, x), exp: 4 (over y, core).
Axes of the slice: x: 2, y: 2, z: 4, core: 2. Of those that a mesh axis runs over, the one named last changes fastest.
Arguments:
- template: bfloat16 [256, 128, 128], P('det'), may hold values from -4 to 4
- template_var: bfloat16 [256, 128, 128], P('det'), may hold values from 2 to 32
- science: bfloat16 [4, 2048, 1024], P('exp', 'det'), may hold values from -10 to 10
- science_var: bfloat16 [4, 2048, 1024], P('exp', 'det'), may hold values from 0.5 to 2
- routes_src: int32 [4, 128], P('exp', 'det'), may hold values from 0 to 7, as said below
- routes_blk: int32 [4, 128], P('exp', 'det'), may hold values from 0 to 31
- stamp_rows: int32 [4, 32], P('exp', 'det'), may hold values from 0 to 128
- stamp_cols: int32 [4, 32], P('exp', 'det'), may hold values from 0 to 896
- basis_col: bfloat16 [40, 21], replicated, may hold values from -1.25 to 1.25
- basis_row: bfloat16 [40, 21], replicated, may hold values from -1.25 to 1.25
- psf_col: float32 [4, 21], P('exp'), may hold values from 0.05 to 0.5
- psf_row: float32 [4, 21], P('exp'), may hold values from 0.05 to 0.5
Outputs:
- significance: float32 [256, 128, 128], P('det')
- psf_score: float32 [4, 2048, 1024], P('exp', 'det')
- coefficients: float32 [4, 328], P('exp', 'det')
Inputs may be any that keep to these rules, and one draw needn't show every extreme that they name: `routes_src`: within the 16 blocks of one device, at most 2 take their template from one owner, and on every device some owner supplies exactly 2 of them.
All inputs are finite; a program needn't handle non-finite values.
Results may differ from a plain program's by a relative error of at most 0.0085.
Values may be sent and summed in bfloat16 or wider, within the bound.
No kernel may reach another device: no remote copies, remote signals or barrier semaphores. Data moves between devices by JAX's collectives and lax.ppermute only.
A program may use at most 128 MiB of HBM per device.

v0:
```python
import jax
import jax.numpy as jnp
from jax import lax
from jax.sharding import PartitionSpec as P

precise_mode = lax.Precision.HIGHEST
ridge_term = 0.01


def band_stack(filters, block_side):
    kernel_taps = filters.shape[1]
    inputs = jnp.arange(block_side + kernel_taps - 1)[:, None, None]
    outputs = jnp.arange(block_side)[None, :, None]
    offsets = jnp.arange(kernel_taps)[None, None, :]
    select = (inputs - outputs == offsets).astype(jnp.float32)
    return jnp.einsum("ni,rvi->nrv", filters.astype(jnp.float32), select, precision=precise_mode)


def column_windows(padded, block_side, kernel_taps):
    height_all, padded_span = padded.shape
    count_blocks = (padded_span - kernel_taps + 1) // block_side
    extended = jnp.pad(padded, ((0, 0), (0, (count_blocks + 1) * block_side - padded_span)))
    tiled_rows = extended.reshape(height_all, count_blocks + 1, block_side)
    return jnp.concatenate(
        [tiled_rows[:, :count_blocks], tiled_rows[:, 1:, : kernel_taps - 1]], axis=2
    )


def row_windows(padded, block_side, kernel_taps):
    padded_span, across = padded.shape
    count_blocks = (padded_span - kernel_taps + 1) // block_side
    extended = jnp.pad(padded, ((0, (count_blocks + 1) * block_side - padded_span), (0, 0)))
    tiled_rows = extended.reshape(count_blocks + 1, block_side, across)
    return jnp.concatenate([tiled_rows[:count_blocks], tiled_rows[1:, : kernel_taps - 1]], axis=1)


def to_image(blocks, block_rows, block_cols):
    block_side = blocks.shape[-1]
    shaped = blocks.reshape(block_rows, block_cols, block_side, block_side).transpose(0, 2, 1, 3)
    return shaped.reshape(block_rows * block_side, block_cols * block_side)


def to_blocks(picture, block_side):
    height_all, across = picture.shape
    shaped = picture.reshape(height_all // block_side, block_side, across // block_side, block_side)
    return shaped.transpose(0, 2, 1, 3).reshape(-1, block_side, block_side)


def fit_kernel(
    frame_img, science_img, variance_img, rows_at, cols_at, basis_col, basis_row, block_side
):
    kernel_taps = basis_col.shape[1]
    margin = kernel_taps // 2
    padded = jnp.pad(frame_img, margin)
    stamp_side = block_side + kernel_taps - 1

    def cut_stamp(top_row, left_col):
        return (
            lax.dynamic_slice(padded, (top_row, left_col), (stamp_side, stamp_side)),
            lax.dynamic_slice(science_img, (top_row, left_col), (block_side, block_side)),
            lax.dynamic_slice(variance_img, (top_row, left_col), (block_side, block_side)),
        )

    stamps, science_cut, variance_cut = jax.vmap(cut_stamp)(rows_at, cols_at)
    col_bands = band_stack(basis_col, block_side).astype(jnp.bfloat16)
    row_bands = band_stack(basis_row, block_side).astype(jnp.bfloat16)
    vertical = jnp.einsum(
        "kru,srx->skux", col_bands, stamps, preferred_element_type=jnp.float32
    ).astype(jnp.bfloat16)
    design = jnp.einsum("skux,kxv->skuv", vertical, row_bands, preferred_element_type=jnp.float32)
    weight = 1.0 / variance_cut.astype(jnp.float32)
    science_f = science_cut.astype(jnp.float32)
    weighted = design * weight[:, None]
    pixel_count = rows_at.shape[0] * block_side * block_side
    gram_matrix = jnp.einsum("skuv,sluv->kl", weighted, design, precision=precise_mode)
    cross_terms = jnp.sum(weighted, axis=(0, 2, 3))
    weight_total = jnp.sum(weight)
    right_basis = jnp.einsum("skuv,suv->k", weighted, science_f, precision=precise_mode)
    right_back = jnp.sum(weight * science_f)
    upper = jnp.concatenate([gram_matrix, cross_terms[:, None]], axis=1)
    lower = jnp.concatenate([cross_terms, weight_total[None]])[None, :]
    normal = jnp.concatenate([upper, lower], axis=0) / pixel_count
    normal = normal + ridge_term * jnp.eye(normal.shape[0], dtype=jnp.float32)
    right_side = jnp.concatenate([right_basis, right_back[None]]) / pixel_count
    factor = jnp.linalg.cholesky(normal)
    return jax.scipy.linalg.cho_solve((factor, True), right_side)


def apply_kernel(frame_img, kernel_bf, block_side):
    kernel_taps = kernel_bf.shape[0]
    height_all = frame_img.shape[0]
    padded = jnp.pad(frame_img, kernel_taps // 2)
    windows = column_windows(padded, block_side, kernel_taps)
    kernel_bands = band_stack(kernel_bf, block_side).astype(jnp.bfloat16)

    def add_row(offset, running):
        row_slab = lax.dynamic_slice_in_dim(windows, offset, height_all, 0)
        return running + jnp.einsum(
            "ycr,rv->ycv", row_slab, kernel_bands[offset], preferred_element_type=jnp.float32
        )

    start = jnp.zeros((height_all, windows.shape[1], block_side), jnp.float32)
    return lax.fori_loop(0, kernel_taps, add_row, start).reshape(height_all, -1)


def correlate_psf(difference, psf_down, psf_across, block_side):
    kernel_taps = psf_down.shape[0]
    margin = kernel_taps // 2
    height_all, across = difference.shape
    data = difference.astype(jnp.float32)
    across_band = band_stack(psf_across[None, :], block_side)[0]
    windows = column_windows(jnp.pad(data, ((0, 0), (margin, margin))), block_side, kernel_taps)
    sideways = jnp.einsum("ycr,rv->ycv", windows, across_band, precision=precise_mode).reshape(
        height_all, across
    )
    down_band = band_stack(psf_down[None, :], block_side)[0]
    stacked = row_windows(jnp.pad(sideways, ((margin, margin), (0, 0))), block_side, kernel_taps)
    return jnp.einsum("brw,ru->buw", stacked, down_band, precision=precise_mode).reshape(
        height_all, across
    )


def local(
    template,
    template_var,
    science,
    science_var,
    routes_src,
    routes_blk,
    stamp_rows,
    stamp_cols,
    basis_col,
    basis_row,
    psf_col,
    psf_row,
):
    peer_count = lax.axis_size("det")
    block_side = template.shape[1]
    tract_blocks = template.shape[0]
    science_img = science[0]
    variance_img = science_var[0]
    block_rows = science_img.shape[0] // block_side
    block_cols = science_img.shape[1] // block_side
    blocks_dev = block_rows * block_cols
    basis_count = basis_col.shape[0]
    capacity = max(2, (blocks_dev + peer_count - 1) // peer_count)
    slot_count = peer_count * capacity
    owner_of = routes_src[0]
    wanted = routes_blk[0]
    owner_hot = (owner_of[:, None] == jnp.arange(peer_count, dtype=jnp.int32)[None, :]).astype(
        jnp.int32
    )
    earlier = jnp.cumsum(owner_hot, axis=0) - owner_hot
    slot_of = owner_of * capacity + jnp.sum(earlier * owner_hot, axis=1)
    slot_hot = (slot_of[:, None] == jnp.arange(slot_count, dtype=jnp.int32)[None, :]).astype(
        jnp.int32
    )
    request = jnp.sum(slot_hot * (wanted[:, None] + 1), axis=0).reshape(peer_count, capacity)
    incoming = lax.all_to_all(request, "det", split_axis=0, concat_axis=0, tiled=True).reshape(
        slot_count
    )
    chosen = jnp.maximum(incoming - 1, 0)
    arrived = lax.all_to_all(template[chosen], "det", split_axis=0, concat_axis=0, tiled=True)
    frame_img = to_image(arrived[slot_of], block_rows, block_cols)
    fitted = fit_kernel(
        frame_img,
        science_img,
        variance_img,
        stamp_rows[0],
        stamp_cols[0],
        basis_col,
        basis_row,
        block_side,
    )
    kernel = jnp.einsum(
        "k,ki,kj->ij",
        fitted[:basis_count],
        basis_col.astype(jnp.float32),
        basis_row.astype(jnp.float32),
        precision=precise_mode,
    )
    kernel_sum = jnp.sum(kernel)
    matched = apply_kernel(frame_img, kernel.astype(jnp.bfloat16), block_side)
    difference = (science_img.astype(jnp.float32) - matched - fitted[basis_count]).astype(
        jnp.bfloat16
    )
    scored = correlate_psf(difference, psf_col[0], psf_row[0], block_side)
    diff_blocks = to_blocks(difference, block_side)
    svar_blocks = to_blocks(variance_img, block_side)
    sender = jnp.sum(slot_hot * jnp.arange(blocks_dev, dtype=jnp.int32)[:, None], axis=0)
    tract_hot = incoming[None, :] - 1 == jnp.arange(tract_blocks, dtype=jnp.int32)[:, None]
    tract_float = tract_hot.astype(jnp.float32)
    back_diff, back_svar = (
        lax.all_to_all(diff_blocks[sender], "det", split_axis=0, concat_axis=0, tiled=True),
        lax.all_to_all(svar_blocks[sender], "det", split_axis=0, concat_axis=0, tiled=True),
    )
    kernel_sums = lax.all_gather(kernel_sum[None], "det", axis=0, tiled=True)
    source_sum = jnp.repeat(kernel_sums, capacity)
    back_var = back_svar.astype(jnp.float32) + (source_sum * source_sum)[
        :, None, None
    ] * template_var[chosen].astype(jnp.float32)
    diff_total = jnp.einsum(
        "mq,qpv->mpv", tract_hot.astype(jnp.bfloat16), back_diff, preferred_element_type=jnp.float32
    )
    var_total = jnp.einsum("mq,qpv->mpv", tract_float, back_var, precision=precise_mode)
    summed_diff, summed_var = (
        lax.psum(diff_total.astype(jnp.bfloat16), "exp").astype(jnp.float32),
        lax.psum(var_total.astype(jnp.bfloat16), "exp").astype(jnp.float32),
    )
    significance = summed_diff / jnp.sqrt(jnp.maximum(summed_var, 1.0))
    return (significance, scored[None], fitted[None])


def solution(mesh):
    placed = (
        P("det", None, None),
        P("det", None, None),
        P("exp", "det", None),
        P("exp", "det", None),
        P("exp", "det"),
        P("exp", "det"),
        P("exp", "det"),
        P("exp", "det"),
        P(),
        P(),
        P("exp", None),
        P("exp", None),
    )
    return jax.shard_map(
        local,
        mesh=mesh,
        in_specs=placed,
        out_specs=(P("det", None, None), P("exp", "det", None), P("exp", "det")),
        check_vma=False,
    )
```

profile of v0, /device:TPU:1, one launch (start us, length us, event | category | flops | bytes accessed | tf_op | source)
XLA Modules:
  0.0 275.3 jit_solution(2738000533745258855)
XLA Ops:
  11.0 6.4 %all-to-all-start = ((s32[8,1,2]{2,1,0:T(1,128)}), s32[8,1,2]{2,1,0:T(1,128)S(1)}, u32[]{:S(2)}, u32[]{:S(2)}) async-start(s32[8,1,2]{2,1,0:T(1,128)} %bitcast.2), calls=%async_computation | async-start | bytes 8192 | tf_op jit(solution)/shard_map/all_to_all | solution.py:159
  19.9 11.3 %while.19 = (s32[]{:T(128)}, bf16[256,1024]{1,0:T(8,128)(2,1)}, s32[4,2]{0,1:T(2,128)S(1)}, bf16[4,128,128]{2,1,0:T(8,128)(2,1)S(1)}, s32[]{:T(128)}) while((s32[]{:T(128)}, bf16[256,1024]{1,0:T(8,128)(2,1)}, s32[4,2]{0,1:T(2,128)S(1)}, bf16[4,128,128]{2,1,0:T(8,128)(2,1)S(1)}, s32[]{:T(128)}) %tuple.118), condition=%wide.while_cond.2, body=%wide.while_body.2.sunk | while | flops 2 | bytes 65645 | solution.py:60
  20.5 2.2 bitcast_dynamic-update-slice_fusion.8
  23.3 2.2 bitcast_dynamic-update-slice_fusion.8
  26.1 2.2 bitcast_dynamic-update-slice_fusion.8
  28.9 2.2 bitcast_dynamic-update-slice_fusion.8
  31.2 7.7 %while.18 = (s32[]{:T(128)}, bf16[256,1024]{1,0:T(8,128)(2,1)S(1)}, s32[4,2]{0,1:T(2,128)S(1)}, bf16[4,128,128]{2,1,0:T(8,128)(2,1)S(1)}, s32[]{:T(128)}) while((s32[]{:T(128)}, bf16[256,1024]{1,0:T(8,128)(2,1)S(1)}, s32[4,2]{0,1:T(2,128)S(1)}, bf16[4,128,128]{2,1,0:T(8,128)(2,1)S(1)}, s32[]{:T(128)}) %tuple.120), condition=%wide.while_cond.1, body=%wide.while_body.1.sunk | while | flops 2 | bytes 65645 | solution.py:61
  42.0 5.4 %all-to-all-start.1 = ((bf16[16,128,128]{2,1,0:T(8,128)(2,1)}), bf16[16,128,128]{2,1,0:T(8,128)(2,1)S(1)}, u32[]{:S(2)}, u32[]{:S(2)}) async-start(bf16[16,128,128]{2,1,0:T(8,128)(2,1)} %gather_fusion), calls=%async_computation.1 | async-start | bytes 1048576 | tf_op jit(solution)/shard_map/all_to_all | solution.py:163
  54.4 6.4 %all-to-all-done.1 = bf16[16,128,128]{2,1,0:T(8,128)(2,1)S(1)} async-done(((bf16[16,128,128]{2,1,0:T(8,128)(2,1)}), bf16[16,128,128]{2,1,0:T(8,128)(2,1)S(1)}, u32[]{:S(2)}, u32[]{:S(2)}) %all-to-all-start.1) | async-done | bytes 524320 | tf_op jit(solution)/shard_map/all_to_all | solution.py:163
  60.7 4.5 %all-to-all-start.3 = ((bf16[16,128,128]{2,1,0:T(8,128)(2,1)}), bf16[16,128,128]{2,1,0:T(8,128)(2,1)}, u32[]{:S(2)}, u32[]{:S(2)}) async-start(bf16[16,128,128]{2,1,0:T(8,128)(2,1)} %gather_fusion.3), calls=%async_computation.3 | async-start | bytes 1048576 | tf_op jit(solution)/shard_map/all_to_all | solution.py:195
  72.6 10.2 %while.17 = (s32[]{:T(128)}, bf16[276,1044]{1,0:T(8,128)(2,1)S(1)}, s32[4,2]{0,1:T(2,128)S(1)}, bf16[4,148,148]{2,1,0:T(8,128)(2,1)}, s32[]{:T(128)}) while((s32[]{:T(128)}, bf16[276,1044]{1,0:T(8,128)(2,1)S(1)}, s32[4,2]{0,1:T(2,128)S(1)}, bf16[4,148,148]{2,1,0:T(8,128)(2,1)}, s32[]{:T(128)}) %tuple.109), condition=%wide.while_cond, body=%wide.while_body.sunk | while | flops 2 | bytes 123265 | solution.py:59
  82.8 10.6 %fusion.86 = (f32[40]{0:T(128)S(1)}, f32[4,40,128,128]{2,3,0,1:T(8,128)}, f32[4,40,128,128]{2,3,0,1:T(8,128)}) fusion(f32[4,128,128]{1,2,0:T(8,128)} %copy.96, bf16[40,148,128,1]{2,0,1,3:T(8,128)(2,1)S(1)} %fusion.22, bf16[4,148,148]{2,1,0:T(8,128)(2,1)} %get-tuple-element.90, bf16[40,148,128,1]{2,0,1,3:T(8,128)(2,1)} %fusion.23), kind=kOutput, calls=%fused_computation.140 | convolution fusion | flops 1681408000 | bytes 24440096 | tf_op jit(solution)/shard_map/skux,kxv->skuv/dot_general | solution.py:70
  93.4 11.9 %copy.97 = f32[4,40,128,128]{3,1,2,0:T(8,128)} copy(f32[4,40,128,128]{2,3,0,1:T(8,128)} %get-tuple-element.214) | data formatting | bytes 20971520 | tf_op jit(solution)/shard_map/mul | solution.py:73
  105.3 12.0 %copy.98 = f32[4,40,128,128]{3,1,2,0:T(8,128)} copy(f32[4,40,128,128]{2,3,0,1:T(8,128)} %get-tuple-element.226) | data formatting | bytes 20971520 | tf_op jit(solution)/shard_map/skux,kxv->skuv/transpose | solution.py:70
  118.1 12.6 %convolution_bitcast_fusion = f32[40,40]{1,0:T(8,128)S(1)} fusion(f32[4,40,128,128]{3,1,2,0:T(8,128)} %copy.97, f32[4,40,128,128]{3,1,2,0:T(8,128)} %copy.98), kind=kOutput, calls=%fused_computation.46 | convolution fusion | flops 1258291200 | bytes 20977920 | tf_op jit(solution)/shard_map/skuv,sluv->kl/dot_general | solution.py:75
  131.0 3.7 %cholesky.16 = f32[41,41]{1,0:T(8,128)S(1)} custom-call(f32[41,41]{1,0:T(8,128)S(1)} %fusion.57), custom_call_target="Cholesky" | custom-call | tf_op jit(solution)/shard_map/jit(cholesky)/cholesky | solution.py:85
  136.1 3.1 %custom-call.10 = f32[1,41,41]{1,2,0:T(8,128)S(1)} custom-call(f32[1,41,41]{2,1,0:T(8,128)S(1)} %fusion.52), custom_call_target="InvertDiagBlocksLowerTriangular" | custom-call | tf_op jit(solution)/shard_map/jit(_cho_solve)/triangular_solve | solution.py:86
  139.2 7.7 %convolution_bitcast_fusion.1 = f32[40]{0:T(128)S(1)} fusion(f32[4,40,128,128]{3,1,2,0:T(8,128)} %copy.97, bf16[4,128,128,1]{2,1,0,3:T(8,128)(2,1)S(1)} %bitcast.217), kind=kOutput, calls=%fused_computation.47 | convolution fusion | flops 31457280 | bytes 10616992 | tf_op jit(solution)/shard_map/skuv,suv->k/dot_general | solution.py:78
  149.5 22.7 %while.20 = (s32[]{:T(128)}, f32[256,8,128]{2,0,1:T(8,128)S(1)}, bf16[276,8,148]{0,2,1:T(8,128)(2,1)S(1)}, bf16[21,148,128]{2,1,0:T(8,128)(2,1)S(1)}, s32[]{:T(128)}, /*index=5*/s32[]{:T(128)}) while((s32[]{:T(128)}, f32[256,8,128]{2,0,1:T(8,128)S(1)}, bf16[276,8,148]{0,2,1:T(8,128)(2,1)S(1)}, ...), condition=%wide.region_9.10_spmd.clone, body=%wide.region_8.9_spmd.clone.sunk | while | flops 78118912 | bytes 2759759 | solution.py:103
  175.7 5.5 %all-to-all-start.2 = ((bf16[16,128,128]{2,1,0:T(8,128)(2,1)}), bf16[16,128,128]{2,1,0:T(8,128)(2,1)S(1)}, u32[]{:S(2)}, u32[]{:S(2)}) async-start(bf16[16,128,128]{2,1,0:T(8,128)(2,1)} %gather_fusion.2), calls=%async_computation.2 | async-start | bytes 1048576 | tf_op jit(solution)/shard_map/all_to_all | solution.py:194
  186.1 18.0 %all-reduce.6 = f32[8]{0:T(128)S(1)} all-reduce(f32[8]{0:T(128)S(1)} %dynamic-update-slice.9), channel_id=1, replica_groups=mesh['det'=8,'exp'=4] {'det'}, use_global_device_ids=true, to_apply=%add.6 | all-reduce | flops 8 | bytes 64
  205.5 2.5 convolution_convert_fusion
  216.3 47.6 %all-reduce.10.cloned.1.call-done = (bf16[32,128,128]{2,0,1:T(8,128)(2,1)}, bf16[32,128,128]{2,0,1:T(8,128)(2,1)}) async-done(((bf16[32,128,128]{2,0,1:T(8,128)(2,1)}, bf16[32,128,128]{2,0,1:T(8,128)(2,1)}), (bf16[32,128,128]{2,0,1:T(8,128)(2,1)}, bf16[32,128,128]{2,0,1:T(8,128)(2,1)})) %all-reduce.10.cloned.1.call-update) | async-done | bytes 2097168 | tf_op jit(solution)/shard_map/psum | solution.py:208
  265.9 2.5 copy.112
  (173 shorter events, 90.9 us)
Async XLA Ops:
  7.2 33.4 %copy-start = (bf16[32,128,128]{2,1,0:T(8,128)(2,1)S(1)}, bf16[32,128,128]{2,1,0:T(8,128)(2,1)}, u32[]{:S(2)}) copy-start(bf16[32,128,128]{2,1,0:T(8,128)(2,1)} %param.14) | copy-start | bytes 3145732
  7.2 24.0 %copy-start.5 = (bf16[1,256,1024]{2,1,0:T(8,128)(2,1)S(1)}, bf16[1,256,1024]{2,1,0:T(8,128)(2,1)}, u32[]{:S(2)}) copy-start(bf16[1,256,1024]{2,1,0:T(8,128)(2,1)} %param.17) | copy-start | bytes 1572868
  11.0 29.5 %all-to-all-start = ((s32[8,1,2]{2,1,0:T(1,128)}), s32[8,1,2]{2,1,0:T(1,128)S(1)}, u32[]{:S(2)}, u32[]{:S(2)}) async-start(s32[8,1,2]{2,1,0:T(1,128)} %bitcast.2), calls=%async_computation | async-start | bytes 8192 | tf_op jit(solution)/shard_map/all_to_all | solution.py:159
  42.0 18.8 %all-to-all-start.1 = ((bf16[16,128,128]{2,1,0:T(8,128)(2,1)}), bf16[16,128,128]{2,1,0:T(8,128)(2,1)S(1)}, u32[]{:S(2)}, u32[]{:S(2)}) async-start(bf16[16,128,128]{2,1,0:T(8,128)(2,1)} %gather_fusion), calls=%async_computation.1 | async-start | bytes 1048576 | tf_op jit(solution)/shard_map/all_to_all | solution.py:163
  49.2 2.7 copy-start.9
  49.2 2.8 copy-start.8
  50.4 2.2 copy-start.7
  60.7 115.0 %all-to-all-start.3 = ((bf16[16,128,128]{2,1,0:T(8,128)(2,1)}), bf16[16,128,128]{2,1,0:T(8,128)(2,1)}, u32[]{:S(2)}, u32[]{:S(2)}) async-start(bf16[16,128,128]{2,1,0:T(8,128)(2,1)} %gather_fusion.3), calls=%async_computation.3 | async-start | bytes 1048576 | tf_op jit(solution)/shard_map/all_to_all | solution.py:195
  146.9 2.4 copy-start.3
  146.9 2.5 copy-start.6
  148.0 24.2 %copy-start.10 = (f32[1,41]{1,0:T(1,128)}, f32[1,41]{1,0:T(1,128)S(1)}, u32[]{:S(2)}) copy-start(f32[1,41]{1,0:T(1,128)S(1)} %fusion.54) | copy-start | bytes 496
  172.2 1.2 copy-start.2
  174.2 7.0 %copy-start.4 = (bf16[256,1024]{1,0:T(8,128)(2,1)S(1)}, bf16[256,1024]{1,0:T(8,128)(2,1)}, u32[]{:S(2)}) copy-start(bf16[256,1024]{1,0:T(8,128)(2,1)} %get-tuple-element.415) | copy-start | bytes 1572868
  174.3 7.2 %copy-start.13 = (u32[32]{0:T(128)S(1)}, u32[32]{0:T(128)}, u32[]{:S(2)}) copy-start(u32[32]{0:T(128)} %constant.188) | copy-start | bytes 388
  174.3 7.7 %copy-start.11 = (f32[1,21]{1,0:T(1,128)S(1)}, f32[1,21]{1,0:T(1,128)}, u32[]{:S(2)}) copy-start(f32[1,21]{1,0:T(1,128)} %param.25) | copy-start | bytes 256
  175.7 32.3 %all-to-all-start.2 = ((bf16[16,128,128]{2,1,0:T(8,128)(2,1)}), bf16[16,128,128]{2,1,0:T(8,128)(2,1)S(1)}, u32[]{:S(2)}, u32[]{:S(2)}) async-start(bf16[16,128,128]{2,1,0:T(8,128)(2,1)} %gather_fusion.2), calls=%async_computation.2 | async-start | bytes 1048576 | tf_op jit(solution)/shard_map/all_to_all | solution.py:194
  181.2 82.8 %all-reduce.10.cloned.1.call-start = ((), (), s32[]{:S(2)}) async-start(), calls=%async_computation.4 | async-start | bytes 4194304 | tf_op jit(solution)/shard_map/psum | solution.py:208
  208.0 1.6 copy-start.12
  263.9 4.5 %copy-start.1 = (bf16[32,128,128]{2,1,0:T(8,128)(2,1)S(1)}, bf16[32,128,128]{2,1,0:T(8,128)(2,1)}, u32[]{:S(2)}) copy-start(bf16[32,128,128]{2,1,0:T(8,128)(2,1)} %param.14) | copy-start | bytes 3145732
Sparse Core Ops, SparseCore 0:
  209.8 54.1 all-reduce.9
where the time goes:
time: 278 us; the launch traced here: 275 us
  local copies, waits for them, and re-layouts  78.7 us (28%)
  matrix products  66.6 us (24%)
  waiting for transfers between devices  54 us (19%)
  starting transfers between devices  21.8 us (8%)
  other arithmetic  21 us (8%)
  blocking collectives  18 us (6%)
  between operations  14.5 us (5%)
    psum x1, waiting for transfers between devices, local(): lax.psum(var_total.astype(jnp.bfloat16), 'exp').astype(jnp.float32)  47.6 us
    gather x36, local copies, waits for them, and re-layouts  29 us
    dot_general x21, matrix products, add_row(): jnp.einsum('ycr,rv->ycv', row_slab, kernel_bands[offset], preferred_eleme...  22.2 us
    unnamed x1, blocking collectives  18 us
    dot_general x1, matrix products, fit_kernel(): jnp.einsum('skuv,sluv->kl', weighted, design, precision=precise_mode)  12.6 us
    transpose x1, local copies, waits for them, and re-layouts, fit_kernel(): jnp.einsum('skux,kxv->skuv', vertical, row_bands, preferred_element_type=...  12 us
    mul x1, local copies, waits for them, and re-layouts, fit_kernel(): weighted = design * weight[:, None]  11.9 us
    dot_general x1, matrix products, fit_kernel(): jnp.einsum('skux,kxv->skuv', vertical, row_bands, preferred_element_type=...  10.6 us
  transfers between devices with their start and end apart: 5, of which 2 were waited for; matrix products, arithmetic and copies ran while one was open for 56% of the time, Pallas kernels for 0%

commit v1 on v0

v1 whole, which is shorter than its diff:
```python
import functools

import jax
import jax.numpy as jnp
from jax import lax
from jax.experimental import pallas as pl
from jax.experimental.pallas import tpu as pltpu
from jax.sharding import PartitionSpec as P

ridge_term = 0.01
bf16 = jnp.bfloat16
f32 = jnp.float32
vmem = functools.partial(pl.BlockSpec, memory_space=pltpu.VMEM)
smem = functools.partial(pl.BlockSpec, memory_space=pltpu.SMEM)
limit = 56 * 1024 * 1024


def up(value, step):
    return -(-value // step) * step


def cost(flops, moved):
    return pl.CostEstimate(flops=flops, bytes_accessed=moved, transcendentals=0)


def route_body(src, blk, request, slot_of, sender, count, *, peers, exps, capacity):
    def clear_count(p, carry):
        count[p] = 0
        return carry

    def clear_slot(s, carry):
        sender[s] = 0
        for e in range(exps):
            request[(s // capacity) * exps + e, 0, s % capacity] = 0
        return carry

    lax.fori_loop(0, peers, clear_count, 0)
    lax.fori_loop(0, peers * capacity, clear_slot, 0)
    for b in range(src.shape[1]):
        owner = src[0, b]
        place = count[owner]
        count[owner] = place + 1
        slot_of[b] = owner * capacity + place
        sender[owner * capacity + place] = b
        for e in range(exps):
            request[owner * exps + e, 0, place] = blk[0, b] + 1


def route_tables(routes_src, routes_blk, peers, exps, capacity):
    body = functools.partial(route_body, peers=peers, exps=exps, capacity=capacity)
    return pl.pallas_call(
        body,
        out_shape=(
            jax.ShapeDtypeStruct((peers * exps, 1, capacity), jnp.int32),
            jax.ShapeDtypeStruct((routes_src.shape[1],), jnp.int32),
            jax.ShapeDtypeStruct((peers * capacity,), jnp.int32),
        ),
        in_specs=[smem()] * 2,
        out_specs=(smem(), smem(), smem()),
        scratch_shapes=[pltpu.SMEM((peers,), jnp.int32)],
        name="route_tables",
    )(routes_src, routes_blk)


def pick_body(incoming, me, template, out, sems, *, exps, capacity):
    slots = out.shape[0]

    def copy(s):
        wanted = incoming[(s // capacity) * exps + me[0], s % capacity]
        block = jnp.maximum(wanted - 1, 0)
        return pltpu.make_async_copy(template.at[block], out.at[s], sems.at[s])

    for s in range(slots):
        copy(s).start()
    for s in range(slots):
        copy(s).wait()


def pick_blocks(incoming, me, template, slots, exps, capacity):
    return pl.pallas_call(
        functools.partial(pick_body, exps=exps, capacity=capacity),
        out_shape=jax.ShapeDtypeStruct((slots,) + template.shape[1:], template.dtype),
        in_specs=[smem(), smem(), pl.BlockSpec(memory_space=pl.ANY)],
        out_specs=pl.BlockSpec(memory_space=pl.ANY),
        scratch_shapes=[pltpu.SemaphoreType.DMA((slots,))],
        name="pick_blocks",
    )(incoming, me, template)


def store_parts(sender, image, out, side, exps, capacity, across_blocks):
    part = side // exps
    slots = sender.shape[0]

    def one(s, carry):
        b = sender[s]
        top = pl.multiple_of((b // across_blocks) * side, side)
        left = pl.multiple_of((b % across_blocks) * side, side)
        block = image[pl.ds(top, side), pl.ds(left, side)].astype(bf16)
        row = pl.multiple_of((s % capacity) * part, part)
        for q in range(exps):
            out[(s // capacity) * exps + q, pl.ds(row, part), :] = block[q * part : (q + 1) * part]
        return carry

    lax.fori_loop(0, slots, one, 0, unroll=True if slots <= 32 else 4)


def send_body(sender, image, out, *, side, exps, capacity, across_blocks):
    store_parts(sender, image, out, side, exps, capacity, across_blocks)


def send_parts(sender, image, side, peers, exps, capacity):
    part = side // exps
    body = functools.partial(
        send_body, side=side, exps=exps, capacity=capacity, across_blocks=image.shape[1] // side
    )
    return pl.pallas_call(
        body,
        out_shape=jax.ShapeDtypeStruct((peers * exps, capacity * part, side), bf16),
        in_specs=[smem(), vmem()],
        out_specs=vmem(),
        compiler_params=pltpu.CompilerParams(vmem_limit_bytes=limit),
        name="send_parts",
    )(sender, image)


def fit_body(
    slot_of,
    sender,
    rows_at,
    cols_at,
    arrived,
    science,
    variance,
    col_bands,
    row_bands,
    col_t,
    row_rev,
    coef_out,
    payload,
    diff_out,
    frame,
    image_f,
    var_f,
    vert,
    design,
    windows,
    bands,
    matched,
    roots,
    *,
    side,
    exps,
    capacity,
    count,
    taps,
):
    high, wide = science.shape
    across_blocks = wide // side
    margin = taps // 2
    stamps = rows_at.shape[1]
    span_r = up(side + taps - 1, 16)
    padded_k = up(count + 2, 16)
    load_r = span_r
    part = side // exps

    frame[...] = jnp.zeros(frame.shape, f32)
    for b in range(slot_of.shape[0]):
        top = margin + (b // across_blocks) * side
        left = margin + (b % across_blocks) * side
        frame[top : top + side, left : left + side] = arrived[slot_of[b]].astype(f32)
    image_f[...] = jnp.zeros(image_f.shape, f32)
    var_f[...] = jnp.ones(var_f.shape, f32)
    image_f[:high, :wide] = science[...].astype(f32)
    var_f[:high, :wide] = variance[...].astype(f32)

    def cut(ref, top, left, height):
        down = pl.multiple_of((top // 8) * 8, 8)
        over = pl.multiple_of((left // side) * side, side)
        tile = ref[pl.ds(down, height), pl.ds(over, 3 * side)]
        tile = pltpu.roll(tile, lax.rem(3 * side - (left - over), 3 * side), 1)[:, : 2 * side]
        return pltpu.roll(tile, lax.rem(height - (top - down), height), 0)

    cuts = []
    for s in range(stamps):
        top = rows_at[0, s]
        left = cols_at[0, s]
        cuts.append(cut(frame, top, left, load_r).astype(bf16))
        science_cut = cut(image_f, top, left, side + 8)[:side, :side]
        weight_root = lax.rsqrt(cut(var_f, top, left, side + 8)[:side, :side])
        design[pl.ds(s * side * padded_k + count, side, stride=padded_k), :] = weight_root
        design[pl.ds(s * side * padded_k + count + 1, side, stride=padded_k), :] = (
            weight_root * science_cut
        )
        for extra in range(count + 2, padded_k):
            design[pl.ds(s * side * padded_k + extra, side, stride=padded_k), :] = jnp.zeros(
                (side, side), f32
            )
        roots[s * side : (s + 1) * side, :] = weight_root

    group = 4
    for k in range(0, count, group):
        filters = col_bands[k * side : (k + group) * side, :]
        for s in range(stamps):
            out = jnp.dot(filters, cuts[s], preferred_element_type=f32).astype(bf16)
            for a in range(group):
                vert[k + a, s * side : (s + 1) * side, :] = out[a * side : (a + 1) * side]

    for k in range(count):
        out = jnp.dot(vert[k], row_bands[k], preferred_element_type=f32)
        design[pl.ds(k, stamps * side, stride=padded_k), :] = out * roots[...]

    lines = 16

    def gram_step(step, total):
        start = pl.multiple_of(step * lines * padded_k, lines * padded_k)
        rows = design[pl.ds(start, lines * padded_k), :]
        tops = []
        lows = []
        for j in range(lines):
            line = rows[j * padded_k : (j + 1) * padded_k]
            top = line.astype(bf16)
            tops.append(top)
            lows.append((line - top.astype(f32)).astype(bf16))
        both = jnp.concatenate(
            [jnp.concatenate(tops, axis=1), jnp.concatenate(lows, axis=1)], axis=0
        )
        return total + lax.dot_general(
            both, both, (((1,), (1,)), ((), ())), preferred_element_type=f32
        )

    gram = lax.fori_loop(
        0, stamps * side // lines, gram_step, jnp.zeros((2 * padded_k, 2 * padded_k), f32)
    )
    folded = gram[:padded_k] + gram[padded_k:]
    folded = jnp.concatenate([folded, jnp.zeros((padded_k, side - 2 * padded_k), f32)], axis=1)
    folded = folded + pltpu.roll(folded, side - padded_k, 1)
    sub = lax.broadcasted_iota(jnp.int32, (padded_k, side), 0)
    lane = lax.broadcasted_iota(jnp.int32, (padded_k, side), 1)
    size = count + 1
    system = folded / (stamps * side * side)
    system = jnp.where((sub < size) & (lane <= size), system, 0.0)
    system = system + jnp.where((sub == lane) & (sub < size), ridge_term, 0.0)

    for k in range(size):
        row = system[k : k + 1, :]
        factor = system[:, k : k + 1] * (1.0 / row[:, k : k + 1])
        factor = jnp.where(sub[:, :1] == k, 0.0, factor)
        system = system - factor * row
    pivot = jnp.sum(jnp.where(sub == lane, system, 0.0), axis=1, keepdims=True)
    solved = system[:, size : size + 1] / jnp.where(sub[:, :1] < size, pivot, 1.0)
    coef_out[...] = jnp.sum(jnp.where(sub == lane, solved, 0.0), axis=0, keepdims=True)
    background = solved[count : count + 1, :]
    basis_coef = jnp.where(sub[:, :1] < count, solved, 0.0)

    scaled = basis_coef * row_rev[...]
    kernel = jnp.zeros((col_t.shape[0], side), f32)
    for _ in range(3):
        piece = scaled.astype(bf16)
        scaled = scaled - piece.astype(f32)
        kernel = kernel + jnp.dot(col_t[...], piece, preferred_element_type=f32)
    kernel_sum = jnp.sum(jnp.sum(kernel, axis=1, keepdims=True), axis=0, keepdims=True)
    rounded = kernel.astype(bf16).astype(f32)

    zero_band = jnp.zeros((side, side), bf16)

    def band(i):
        if i < 0 or i >= taps:
            return zero_band
        line = jnp.broadcast_to(rounded[i : i + 1, :], (side, side))
        return pltpu.roll(line, 0, 1, stride=1, stride_axis=0).astype(bf16)

    pairs = (taps + 2) // 2
    made = {i: band(i) for i in range(-1, 2 * pairs)}
    for q in range(pairs):
        for a in range(2):
            for b in range(2):
                bands[
                    q * 2 * side + a * side : q * 2 * side + (a + 1) * side,
                    b * side : (b + 1) * side,
                ] = made[2 * q + a - b]

    step = side - taps + 1
    rows_half = high // 2
    for c in range(windows.shape[0]):
        windows[c] = frame[:, c * step : c * step + side]
    for c in range(windows.shape[0]):
        lhs = jnp.concatenate(
            [
                windows[c, pl.ds(row, rows_half, stride=2), :].astype(bf16)
                for row in range(2 * pairs)
            ],
            axis=1,
        )
        out = jnp.dot(lhs, bands[...], preferred_element_type=f32)
        windows[c, pl.ds(0, rows_half, stride=2), :] = out[:, :side]
        windows[c, pl.ds(1, rows_half, stride=2), :] = out[:, side:]
        keep = min(step, wide - c * step)
        matched[:, c * step : c * step + keep] = windows[c, :high, :keep]
    image_f[:high, :wide] = image_f[:high, :wide] - matched[:, :wide] - background
    difference = image_f[:high, :wide].astype(bf16)
    diff_out[...] = difference

    store_parts(sender, diff_out, payload, side, exps, capacity, across_blocks)
    line_at = lax.broadcasted_iota(jnp.int32, (16, side), 0)
    trailer = jnp.zeros((16, side), f32)
    rest = kernel_sum
    for p in range(3):
        piece = rest.astype(bf16).astype(f32)
        rest = rest - piece
        trailer = jnp.where(line_at == p, piece, trailer)
    trailer = trailer.astype(bf16)

    def put(d, carry):
        payload[d, capacity * part :, :] = trailer
        return carry

    lax.fori_loop(0, payload.shape[0], put, 0, unroll=4)


def fit_and_subtract(
    slot_of,
    sender,
    rows_at,
    cols_at,
    arrived,
    science,
    variance,
    col_bands,
    row_bands,
    col_t,
    row_rev,
    peers,
    exps,
    capacity,
    count,
    taps,
):
    side = arrived.shape[1]
    high, wide = science.shape
    stamps = rows_at.shape[1]
    padded_k = up(count + 2, 16)
    part = side // exps
    pairs = (taps + 2) // 2
    step = side - taps + 1
    wins = -(-wide // step)
    tall = up(high - side + 8 + up(side + taps - 1, 16), 16)
    tall = max(tall, up(high + 2 * pairs, 16))
    broad = wide + 2 * side
    body = functools.partial(
        fit_body, side=side, exps=exps, capacity=capacity, count=count, taps=taps
    )
    return pl.pallas_call(
        body,
        out_shape=(
            jax.ShapeDtypeStruct((1, side), f32),
            jax.ShapeDtypeStruct((peers * exps, capacity * part + 16, side), bf16),
            jax.ShapeDtypeStruct((high, wide), bf16),
        ),
        in_specs=[smem()] * 4 + [vmem()] * 7,
        out_specs=(vmem(), vmem(), vmem()),
        scratch_shapes=[
            pltpu.VMEM((tall, broad), f32),
            pltpu.VMEM((high + 8, broad), f32),
            pltpu.VMEM((high + 8, broad), f32),
            pltpu.VMEM((count, stamps * side, 2 * side), bf16),
            pltpu.VMEM((stamps * side * padded_k, side), f32),
            pltpu.VMEM((wins, tall, side), f32),
            pltpu.VMEM((pairs * 2 * side, 2 * side), bf16),
            pltpu.VMEM((high, wide), f32),
            pltpu.VMEM((stamps * side, side), f32),
        ],
        compiler_params=pltpu.CompilerParams(vmem_limit_bytes=limit),
        cost_estimate=cost(5_000_000_000, 8_000_000),
        name="fit_and_subtract",
    )(
        slot_of,
        sender,
        rows_at,
        cols_at,
        arrived,
        science,
        variance,
        col_bands,
        row_bands,
        col_t,
        row_rev,
    )


def split2(value):
    top = value.astype(bf16)
    return top, (value - top.astype(f32)).astype(bf16)


def psf_body(diff, down, over, out, padded, sideways, *, side, taps):
    high, wide = diff.shape
    margin = taps // 2
    span = up(side + taps - 1, 16)
    padded[...] = jnp.zeros(padded.shape, f32)
    padded[:, margin : margin + wide] = diff[...].astype(f32)
    line = jnp.broadcast_to(over[...], (2 * side, 2 * side))
    band = pltpu.roll(line, 0, 1, stride=1, stride_axis=0)[:, :side]
    both = jnp.concatenate(split2(band), axis=1)
    sideways[...] = jnp.zeros(sideways.shape, f32)
    for c in range(wide // side):
        window = padded[:, c * side : (c + 2) * side].astype(bf16)
        got = jnp.dot(window, both, preferred_element_type=f32)
        sideways[margin : margin + high, c * side : (c + 1) * side] = got[:, :side] + got[:, side:]
    line = jnp.broadcast_to(down[...], (side, 2 * side))
    band = pltpu.roll(line, 0, 1, stride=1, stride_axis=0)[:, :span]
    top, low = split2(band)
    for r in range(high // side):
        data_top, data_low = split2(sideways[r * side : r * side + span, :])
        got = jnp.dot(top, data_top, preferred_element_type=f32)
        got = got + jnp.dot(top, data_low, preferred_element_type=f32)
        got = got + jnp.dot(low, data_top, preferred_element_type=f32)
        out[r * side : (r + 1) * side, :] = got


def correlate(diff, down, over_rev, side, taps):
    high, wide = diff.shape
    span = up(side + taps - 1, 16)
    return pl.pallas_call(
        functools.partial(psf_body, side=side, taps=taps),
        out_shape=jax.ShapeDtypeStruct((high, wide), f32),
        in_specs=[vmem()] * 3,
        out_specs=vmem(),
        scratch_shapes=[
            pltpu.VMEM((high, wide + side), f32),
            pltpu.VMEM((high - side + span, wide), f32),
        ],
        compiler_params=pltpu.CompilerParams(vmem_limit_bytes=limit),
        cost_estimate=cost(2_000_000_000, 2_000_000),
        name="correlate",
    )(diff, down, over_rev)


def variance_body(incoming, parts, out, *, part, capacity):
    out[...] = jnp.zeros(out.shape, f32)

    def one(j, carry):
        block = incoming[j // capacity, j % capacity] - 1

        @pl.when(block >= 0)
        def _():
            row = pl.multiple_of((j % capacity) * part, part)
            out[block] += parts[j // capacity, pl.ds(row, part), :].astype(f32)

        return carry

    lax.fori_loop(0, parts.shape[0] * capacity, one, 0)


def sum_variance(incoming, parts, tract, part, capacity):
    return pl.pallas_call(
        functools.partial(variance_body, part=part, capacity=capacity),
        out_shape=jax.ShapeDtypeStruct((tract, part, parts.shape[2]), f32),
        in_specs=[smem(), vmem()],
        out_specs=vmem(),
        compiler_params=pltpu.CompilerParams(vmem_limit_bytes=limit),
        name="sum_variance",
    )(incoming, parts)


def combine_body(incoming, parts, var_sum, var_template, out, total, gain, *, part, capacity):
    total[...] = jnp.zeros(total.shape, f32)
    gain[...] = jnp.zeros(gain.shape, f32)

    def one(j, carry):
        block = incoming[j // capacity, j % capacity] - 1

        @pl.when(block >= 0)
        def _():
            row = pl.multiple_of((j % capacity) * part, part)
            total[block] += parts[j // capacity, pl.ds(row, part), :].astype(f32)
            tail = parts[j // capacity, capacity * part :, :].astype(f32)
            kernel_sum = tail[0:1] + tail[1:2] + tail[2:3]
            gain[block] += jnp.broadcast_to(kernel_sum * kernel_sum, gain.shape[1:])

        return carry

    lax.fori_loop(0, parts.shape[0] * capacity, one, 0)
    for t in range(out.shape[0]):
        variance = var_sum[t] + gain[t, 0:1, :] * var_template[t].astype(f32)
        out[t] = (total[t] * lax.rsqrt(jnp.maximum(variance, 1.0))).astype(bf16)


def combine(incoming, parts, var_sum, var_template, part, capacity):
    tract, _, side = var_sum.shape
    return pl.pallas_call(
        functools.partial(combine_body, part=part, capacity=capacity),
        out_shape=jax.ShapeDtypeStruct((tract, part, side), bf16),
        in_specs=[smem(), vmem(), vmem(), vmem()],
        out_specs=vmem(),
        scratch_shapes=[
            pltpu.VMEM((tract, part, side), f32),
            pltpu.VMEM((tract, 8, side), f32),
        ],
        compiler_params=pltpu.CompilerParams(vmem_limit_bytes=limit),
        name="combine",
    )(incoming, parts, var_sum, var_template)


def join_body(places, *refs, part):
    out = refs[-1]
    for d, ref in enumerate(refs[:-1]):
        row = pl.multiple_of(places[d] * part, part)
        out[:, pl.ds(row, part), :] = ref[...].astype(f32)


def join_parts(places, parts):
    tract, part, side = parts[0].shape
    exps = len(parts)
    chunk = 8
    grid_spec = pltpu.PrefetchScalarGridSpec(
        num_scalar_prefetch=1,
        grid=(tract // chunk,),
        in_specs=[pl.BlockSpec((chunk, part, side), lambda i, _: (i, 0, 0))] * exps,
        out_specs=pl.BlockSpec((chunk, part * exps, side), lambda i, _: (i, 0, 0)),
    )
    return pl.pallas_call(
        functools.partial(join_body, part=part),
        out_shape=jax.ShapeDtypeStruct((tract, part * exps, side), f32),
        grid_spec=grid_spec,
        name="join_parts",
    )(places, *parts)


def local(
    template,
    template_var,
    science,
    science_var,
    routes_src,
    routes_blk,
    stamp_rows,
    stamp_cols,
    basis_col,
    basis_row,
    psf_col,
    psf_row,
):
    peers = lax.axis_size("det")
    exps = lax.axis_size("exp")
    me = lax.axis_index("exp").astype(jnp.int32)
    tract, side, _ = template.shape
    science_img = science[0]
    variance_img = science_var[0]
    blocks_dev = routes_src.shape[1]
    count, taps = basis_col.shape
    capacity = max(2, -(-blocks_dev // peers))
    slots = peers * capacity
    part = side // exps

    request, slot_of, sender = route_tables(routes_src, routes_blk, peers, exps, capacity)
    incoming = lax.all_to_all(
        request, ("det", "exp"), split_axis=0, concat_axis=0, tiled=True
    ).reshape(peers * exps, capacity)
    picked = pick_blocks(incoming, me[None], template, slots, exps, capacity)
    arrived = lax.all_to_all(picked, "det", split_axis=0, concat_axis=0, tiled=True)

    span = up(side + taps - 1, 16)
    padded_k = up(count + 2, 16)
    offset = jnp.arange(span)[None, :] - jnp.arange(side)[:, None]
    hot = (offset[:, :, None] == jnp.arange(taps)).astype(bf16)
    col_bands = jnp.einsum("ki,uri->kur", basis_col, hot, preferred_element_type=f32)
    col_bands = col_bands.astype(bf16).reshape(count * side, span)
    offset = jnp.arange(2 * side)[:, None] - jnp.arange(side)[None, :]
    hot = (offset[:, :, None] == jnp.arange(taps)).astype(bf16)
    row_bands = jnp.einsum("kj,xvj->kxv", basis_row, hot, preferred_element_type=f32)
    row_bands = row_bands.astype(bf16)
    col_t = jnp.pad(basis_col.T, ((0, up(taps, 16) - taps), (0, padded_k - count)))
    row_rev = jnp.pad(
        basis_row.astype(f32)[:, ::-1], ((0, padded_k - count), (side - taps, 0))
    )
    row_rev = jnp.roll(row_rev, 1, axis=1)
    over_rev = jnp.roll(jnp.pad(psf_row[:, ::-1], ((0, 0), (2 * side - taps, 0))), 1, axis=1)
    down = jnp.pad(psf_col, ((0, 0), (0, 2 * side - taps)))

    var_parts = send_parts(sender, variance_img, side, peers, exps, capacity)
    var_back = lax.all_to_all(
        var_parts, ("det", "exp"), split_axis=0, concat_axis=0, tiled=True
    )

    coef, payload, difference = fit_and_subtract(
        slot_of,
        sender,
        stamp_rows,
        stamp_cols,
        arrived,
        science_img,
        variance_img,
        col_bands,
        row_bands,
        col_t,
        row_rev,
        peers,
        exps,
        capacity,
        count,
        taps,
    )
    diff_back = lax.all_to_all(payload, ("det", "exp"), split_axis=0, concat_axis=0, tiled=True)
    scored = correlate(difference, down, over_rev, side, taps)
    var_sum = sum_variance(incoming, var_back, tract, part, capacity)
    var_template = lax.dynamic_slice_in_dim(template_var, me * part, part, 1)
    mine = combine(incoming, diff_back, var_sum, var_template, part, capacity)

    if exps & (exps - 1) == 0:
        held = [mine]
        reach = exps // 2
        gaps = [0]
        while reach:
            pairs = [(e, e ^ reach) for e in range(exps)]
            held = held + [lax.ppermute(h, "exp", pairs) for h in held]
            gaps = gaps + [g ^ reach for g in gaps]
            reach //= 2
        places = jnp.stack([me ^ g for g in gaps])
    else:
        held = [mine]
        for gap in range(1, exps):
            pairs = [(e, (e + gap) % exps) for e in range(exps)]
            held.append(lax.ppermute(mine, "exp", pairs))
        places = jnp.stack([(me - g) % exps for g in range(exps)])
    significance = join_parts(places, held)
    return (significance, scored[None], coef[:, : count + 1])


def solution(mesh):
    placed = (
        P("det", None, None),
        P("det", None, None),
        P("exp", "det", None),
        P("exp", "det", None),
        P("exp", "det"),
        P("exp", "det"),
        P("exp", "det"),
        P("exp", "det"),
        P(),
        P(),
        P("exp", None),
        P("exp", None),
    )
    return jax.shard_map(
        local,
        mesh=mesh,
        in_specs=placed,
        out_specs=(P("det", None, None), P("exp", "det", None), P("exp", "det")),
        check_vma=False,
    )
```

time: 278 us -> 140 us (0.50)
  local copies, waits for them, and re-layouts: 78.7 us -> 13.4 us
  matrix products: 66.6 us -> 1.58 us
  Pallas kernels: 0 us -> 64.8 us
  waiting for transfers between devices: 54 us -> 32.9 us
  other arithmetic: 21 us -> 1.93 us
  blocking collectives: 18 us -> 0 us
  between operations: 14.5 us -> 0.81 us
    pallas_call x0 -> x8, Pallas kernels: none -> 64.8 us  [the longest x1 28.1 us: fit_and_subtract(): pl.pallas_call(body, out_shape=(jax.ShapeDtypeStruct((1, side), f32), jax...]
    dot_general x34 -> x2, matrix products: 65.5 us -> 1.58 us  [the longest x1 0.92 us: local(): jnp.einsum('kj,xvj->kxv', basis_row, hot, preferred_element_type=f32)]
    psum x1 -> x0, waiting for transfers between devices: 47.6 us -> none  [local(): lax.psum(var_total.astype(jnp.bfloat16), 'exp').astype(jnp.float32)]
    gather x41 -> x0, local copies, waits for them, and re-layouts: 36.5 us -> none
    all_to_all x4, waiting for transfers between devices: 6.38 us -> 28.5 us  [the longest x1 13.5 us: local(): lax.all_to_all(payload, ('det', 'exp'), split_axis=0, concat_axis=0, tile...]
    unnamed x1 -> x0, blocking collectives: 18 us -> none
    transpose x4 -> x0, local copies, waits for them, and re-layouts: 12.2 us -> none  [the longest x1 12 us: fit_kernel(): jnp.einsum('skux,kxv->skuv', vertical, row_bands, preferred_element_type=...]
    mul x2 -> x0, local copies, waits for them, and re-layouts: 12 us -> none  [the longest x1 11.9 us: fit_kernel(): weighted = design * weight[:, None]]
  transfers between devices with their start and end apart: 5 -> 7, of which waited for: 2 -> 4; matrix products, arithmetic and copies ran while one was open for 56% -> 9% of each run, Pallas kernels for 0% -> 26%
where the time goes in v1:
time: 140 us; the launch traced here: 139 us
  Pallas kernels  64.8 us (46%)
  waiting for transfers between devices  32.9 us (24%)
  starting transfers between devices  23.8 us (17%)
  local copies, waits for them, and re-layouts  13.4 us (10%)
  other arithmetic  1.93 us (1%)
  matrix products  1.58 us (1%)
    pallas_call x1, Pallas kernels, fit_and_subtract(): pl.pallas_call(body, out_shape=(jax.ShapeDtypeStruct((1, side), f32), jax...  28.1 us
    pallas_call x1, Pallas kernels, pick_blocks(): pl.pallas_call(functools.partial(pick_body, exps=exps, capacity=capacity)...  18.1 us
    all_to_all x1, waiting for transfers between devices, local(): lax.all_to_all(payload, ('det', 'exp'), split_axis=0, concat_axis=0, tile...  13.5 us
    all_to_all x1, waiting for transfers between devices, local(): lax.all_to_all(picked, 'det', split_axis=0, concat_axis=0, tiled=True)  8.25 us
    all_to_all x1, starting transfers between devices, local(): lax.all_to_all(request, ('det', 'exp'), split_axis=0, concat_axis=0, tile...  7.1 us
    all_to_all x1, waiting for transfers between devices, local(): lax.all_to_all(request, ('det', 'exp'), split_axis=0, concat_axis=0, tile...  6.69 us
    all_to_all x1, starting transfers between devices, local(): lax.all_to_all(payload, ('det', 'exp'), split_axis=0, concat_axis=0, tile...  5.83 us
    convert_element_type x1, local copies, waits for them, and re-layouts, local(): col_bands = col_bands.astype(bf16).reshape(count * side, span)  5.09 us
  transfers between devices with their start and end apart: 7, of which 4 were waited for; matrix products, arithmetic and copies ran while one was open for 9% of the time, Pallas kernels for 26%

profile of v1, /device:TPU:1, one launch (start us, length us, event | category | flops | bytes accessed | tf_op | source)
XLA Modules:
  0.0 139.3 jit_solution(5384926118516687601)
XLA Ops:
  0.7 2.0 %route_tables.1 = (s32[32,1,2]{2,1,0:T(1,128)}, s32[16]{0:T(128)}, s32[16]{0:T(128)}) custom-call(s32[1,16]{1,0:T(1,128)} %src.1, s32[1,16]{1,0:T(1,128)} %blk.1), custom_call_target="tpu_custom_call" | custom-call | tf_op jit(solution)/shard_map/route_tables/pallas_call | solution.py:51
  2.6 7.1 %all-to-all-start = ((s32[32,1,2]{2,1,0:T(1,128)}), s32[32,1,2]{2,1,0:T(1,128)S(1)}, u32[]{:S(2)}, u32[]{:S(2)}) async-start(s32[32,1,2]{2,1,0:T(1,128)} %get-tuple-element.9), calls=%async_computation | async-start | bytes 32768 | tf_op jit(solution)/shard_map/all_to_all | solution.py:556
  9.7 6.7 %all-to-all-done = s32[32,1,2]{2,1,0:T(1,128)S(1)} async-done(((s32[32,1,2]{2,1,0:T(1,128)}), s32[32,1,2]{2,1,0:T(1,128)S(1)}, u32[]{:S(2)}, u32[]{:S(2)}) %all-to-all-start) | async-done | bytes 288 | tf_op jit(solution)/shard_map/all_to_all | solution.py:556
  17.2 18.1 %pick_blocks.1 = bf16[16,128,128]{2,1,0:T(8,128)(2,1)} custom-call(s32[32,2]{1,0:T(8,128)} %copy.28.incoming, s32[1]{0:T(128)} %bitcast.me, bf16[32,128,128]{2,1,0:T(8,128)(2,1)} %template.1), custom_call_target="tpu_custom_call" | custom-call | tf_op jit(solution)/shard_map/pick_blocks/pallas_call | solution.py:80
  35.3 3.5 %all-to-all-start.1 = ((bf16[16,128,128]{2,1,0:T(8,128)(2,1)}), bf16[16,128,128]{2,1,0:T(8,128)(2,1)S(1)}, u32[]{:S(2)}, u32[]{:S(2)}) async-start(bf16[16,128,128]{2,1,0:T(8,128)(2,1)} %pick_blocks.1), calls=%async_computation.1 | async-start | bytes 1048576 | tf_op jit(solution)/shard_map/all_to_all | solution.py:560
  39.0 0.9 fusion
  39.9 2.1 %copy.32 = bf16[256,128,40]{1,0,2:T(8,128)(2,1)} copy(bf16[256,128,40]{1,2,0:T(8,128)(2,1)S(1)} %fusion) | data formatting | bytes 5242880 | tf_op jit(solution)/shard_map/kj,xvj->kxv/dot_general | solution.py:570
  42.1 2.0 %send_parts.1 = bf16[32,64,128]{2,1,0:T(8,128)(2,1)} custom-call(s32[16]{0:T(128)} %get-tuple-element.11.sender, bf16[256,1024]{1,0:T(8,128)(2,1)} %bitcast.25), custom_call_target="tpu_custom_call" | custom-call | tf_op jit(solution)/shard_map/send_parts/pallas_call | solution.py:116
  44.1 8.3 %all-to-all-done.1.arrived = bf16[16,128,128]{2,1,0:T(8,128)(2,1)S(1)} async-done(((bf16[16,128,128]{2,1,0:T(8,128)(2,1)}), bf16[16,128,128]{2,1,0:T(8,128)(2,1)S(1)}, u32[]{:S(2)}, u32[]{:S(2)}) %all-to-all-start.1) | async-done | bytes 524320 | tf_op jit(solution)/shard_map/all_to_all | solution.py:560
  52.3 0.8 copy-done.3
  53.1 4.3 %all-to-all-start.3 = ((bf16[32,64,128]{2,1,0:T(8,128)(2,1)}), bf16[32,64,128]{2,1,0:T(8,128)(2,1)S(1)}, u32[]{:S(2)}, u32[]{:S(2)}) async-start(bf16[32,64,128]{2,1,0:T(8,128)(2,1)} %send_parts.1), calls=%async_computation.3 | async-start | bytes 1048576 | tf_op jit(solution)/shard_map/all_to_all | solution.py:581
  58.1 5.1 %copy.24 = bf16[40,128,160]{2,1,0:T(8,128)(2,1)} copy(bf16[40,128,160]{1,0,2:T(8,128)(2,1)S(1)} %fusion.5) | data formatting | bytes 3276800 | tf_op jit(solution)/shard_map/convert_element_type | solution.py:567
  64.6 28.1 %fit_and_subtract.1 = (f32[1,128]{1,0:T(1,128)}, bf16[32,80,128]{2,1,0:T(8,128)(2,1)}, bf16[256,1024]{1,0:T(8,128)(2,1)}) custom-call(s32[16]{0:T(128)} %get-tuple-element.10.slot_of, s32[16]{0:T(128)} %get-tuple-element.11.sender, s32[1,4]{1,0:T(1,128)} %rows_at.1, s32[1,4]{1,0:T(1,128)} %cols_at.1, bf16[16,128,128]{2,1,0:T(8,128)(2,1)} %copy-done.3, ...), custom_call_target="tpu_custom_call" | custom-call | flops 5000000000 | bytes 8000000 | tf_op jit(solution)/shard_map/fit_and_subtract/pallas_call | solution.py:352
  92.7 5.8 %all-to-all-start.2 = ((bf16[32,80,128]{2,1,0:T(8,128)(2,1)}), bf16[32,80,128]{2,1,0:T(8,128)(2,1)S(1)}, u32[]{:S(2)}, u32[]{:S(2)}) async-start(bf16[32,80,128]{2,1,0:T(8,128)(2,1)} %get-tuple-element.12), calls=%async_computation.2 | async-start | bytes 1310720 | tf_op jit(solution)/shard_map/all_to_all | solution.py:603
  98.6 0.7 constant_dynamic-slice_fusion.var_template
  99.3 3.5 %sum_variance.1.var_sum = f32[32,32,128]{2,1,0:T(8,128)} custom-call(s32[32,2]{1,0:T(8,128)} %copy.28.incoming, bf16[32,64,128]{2,1,0:T(8,128)(2,1)} %copy-done.2), custom_call_target="tpu_custom_call" | custom-call | tf_op jit(solution)/shard_map/sum_variance/pallas_call | solution.py:455
  102.8 13.5 %all-to-all-done.2.parts = bf16[32,80,128]{2,1,0:T(8,128)(2,1)S(1)} async-done(((bf16[32,80,128]{2,1,0:T(8,128)(2,1)}), bf16[32,80,128]{2,1,0:T(8,128)(2,1)S(1)}, u32[]{:S(2)}, u32[]{:S(2)}) %all-to-all-start.2) | async-done | bytes 655392 | tf_op jit(solution)/shard_map/all_to_all | solution.py:603
  116.3 0.8 copy-done.1
  117.1 4.0 %combine.1.refs_0_ = bf16[32,32,128]{2,1,0:T(8,128)(2,1)} custom-call(s32[32,2]{1,0:T(8,128)} %copy.28.incoming, bf16[32,80,128]{2,1,0:T(8,128)(2,1)} %copy-done.1, f32[32,32,128]{2,1,0:T(8,128)} %sum_variance.1.var_sum, bf16[32,32,128]{2,1,0:T(8,128)(2,1)} %constant_dynamic-slice_fusion.var_template), custom_call_target="tpu_custom_call" | custom-call | tf_op jit(solution)/shard_map/combine/pallas_call | solution.py:490
  121.1 1.3 collective-permute-start
  124.3 4.4 %collective-permute-done.refs_1_ = bf16[32,32,128]{2,1,0:T(8,128)(2,1)S(1)} collective-permute-done((bf16[32,32,128]{2,1,0:T(8,128)(2,1)}, bf16[32,32,128]{2,1,0:T(8,128)(2,1)S(1)}, u32[]{:S(2)}, u32[]{:S(2)}) %collective-permute-start) | collective-permute-done | bytes 262176 | tf_op jit(solution)/shard_map/ppermute | solution.py:615
  128.7 1.3 collective-permute-start.2
  130.6 3.1 %correlate.1 = f32[256,1024]{1,0:T(8,128)} custom-call(bf16[256,1024]{1,0:T(8,128)(2,1)} %get-tuple-element.13.diff, f32[1,256]{1,0:T(1,128)} %pad.18.down, f32[1,256]{1,0:T(1,128)} %pad_maximum_fusion.1.over), custom_call_target="tpu_custom_call" | custom-call | flops 2000000000 | bytes 2000000 | tf_op jit(solution)/shard_map/correlate/pallas_call | solution.py:423
  135.1 4.2 %join_parts.1 = f32[32,128,128]{2,1,0:T(8,128)} custom-call(s32[4]{0:T(128)} %pad_add_fusion.places, bf16[32,32,128]{2,1,0:T(8,128)(2,1)} %combine.1.refs_0_, bf16[32,32,128]{2,1,0:T(8,128)(2,1)} %copy-done.4, bf16[32,32,128]{2,1,0:T(8,128)(2,1)} %copy-done.5, bf16[32,32,128]{2,1,0:T(8,128)(2,1)} %copy-done.6), custom_call_target="tpu_custom_call" | custom-call | tf_op jit(solution)/shard_map/join_parts/pallas_call | solution.py:521
  (40 shorter events, 6.9 us)
Async XLA Ops:
  0.6 97.9 %copy-start = (bf16[32,128,128]{2,1,0:T(8,128)(2,1)S(1)}, bf16[32,128,128]{2,1,0:T(8,128)(2,1)}, u32[]{:S(2)}) copy-start(bf16[32,128,128]{2,1,0:T(8,128)(2,1)} %param.13) | copy-start | bytes 3145732
  0.6 38.1 %copy-start.8 = (bf16[40,21]{0,1:T(8,128)(2,1)S(1)}, bf16[40,21]{0,1:T(8,128)(2,1)}, u32[]{:S(2)}) copy-start(bf16[40,21]{0,1:T(8,128)(2,1)} %param.21) | copy-start | bytes 5044
  2.6 13.8 %all-to-all-start = ((s32[32,1,2]{2,1,0:T(1,128)}), s32[32,1,2]{2,1,0:T(1,128)S(1)}, u32[]{:S(2)}, u32[]{:S(2)}) async-start(s32[32,1,2]{2,1,0:T(1,128)} %get-tuple-element.9), calls=%async_computation | async-start | bytes 32768 | tf_op jit(solution)/shard_map/all_to_all | solution.py:556
  35.3 17.1 %all-to-all-start.1 = ((bf16[16,128,128]{2,1,0:T(8,128)(2,1)}), bf16[16,128,128]{2,1,0:T(8,128)(2,1)S(1)}, u32[]{:S(2)}, u32[]{:S(2)}) async-start(bf16[16,128,128]{2,1,0:T(8,128)(2,1)} %pick_blocks.1), calls=%async_computation.1 | async-start | bytes 1048576 | tf_op jit(solution)/shard_map/all_to_all | solution.py:560
  39.9 17.5 %copy-start.7 = (bf16[40,21]{0,1:T(8,128)(2,1)S(1)}, bf16[40,21]{0,1:T(8,128)(2,1)}, u32[]{:S(2)}) copy-start(bf16[40,21]{0,1:T(8,128)(2,1)} %param.20) | copy-start | bytes 5044
  52.3 0.8 copy-start.3
  53.1 39.6 %all-to-all-start.3 = ((bf16[32,64,128]{2,1,0:T(8,128)(2,1)}), bf16[32,64,128]{2,1,0:T(8,128)(2,1)S(1)}, u32[]{:S(2)}, u32[]{:S(2)}) async-start(bf16[32,64,128]{2,1,0:T(8,128)(2,1)} %send_parts.1), calls=%async_computation.3 | async-start | bytes 1048576 | tf_op jit(solution)/shard_map/all_to_all | solution.py:581
  92.7 29.7 %copy-start.9 = (f32[1,21]{1,0:T(1,128)S(1)}, f32[1,21]{1,0:T(1,128)}, u32[]{:S(2)}) copy-start(f32[1,21]{1,0:T(1,128)} %param.23) | copy-start | bytes 256
  92.7 29.8 %copy-start.10 = (f32[1,21]{1,0:T(1,128)S(1)}, f32[1,21]{1,0:T(1,128)}, u32[]{:S(2)}) copy-start(f32[1,21]{1,0:T(1,128)} %param.22) | copy-start | bytes 256
  92.7 6.6 %copy-start.2 = (bf16[32,64,128]{2,1,0:T(8,128)(2,1)}, bf16[32,64,128]{2,1,0:T(8,128)(2,1)S(1)}, u32[]{:S(2)}) copy-start(bf16[32,64,128]{2,1,0:T(8,128)(2,1)S(1)} %all-to-all-done.3.parts) | copy-start | bytes 1572868
  92.7 23.6 %all-to-all-start.2 = ((bf16[32,80,128]{2,1,0:T(8,128)(2,1)}), bf16[32,80,128]{2,1,0:T(8,128)(2,1)S(1)}, u32[]{:S(2)}, u32[]{:S(2)}) async-start(bf16[32,80,128]{2,1,0:T(8,128)(2,1)} %get-tuple-element.12), calls=%async_computation.2 | async-start | bytes 1310720 | tf_op jit(solution)/shard_map/all_to_all | solution.py:603
  116.3 0.8 copy-start.1
  121.1 7.6 %collective-permute-start = (bf16[32,32,128]{2,1,0:T(8,128)(2,1)}, bf16[32,32,128]{2,1,0:T(8,128)(2,1)S(1)}, u32[]{:S(2)}, u32[]{:S(2)}) collective-permute-start(bf16[32,32,128]{2,1,0:T(8,128)(2,1)} %combine.1.refs_0_), channel_id=1, source_target_pairs={{0,2},{1,3},{2,0},{3,1},{4,6},{5,7},{6,4},{7,5},{8,10},{9,11},{10,... | collective-permute-start | bytes 786440 | tf_op jit(solution)/shard_map/ppermute | solution.py:615
  123.8 9.9 %collective-permute-start.1 = (bf16[32,32,128]{2,1,0:T(8,128)(2,1)}, bf16[32,32,128]{2,1,0:T(8,128)(2,1)S(1)}, u32[]{:S(2)}, u32[]{:S(2)}) collective-permute-start(bf16[32,32,128]{2,1,0:T(8,128)(2,1)} %combine.1.refs_0_), channel_id=1, source_target_pairs={{0,1},{1,0},{2,3},{3,2},{4,5},{5,4},{6,7},{7,6},{8,9},{9,8},{10,11... | collective-permute-start | bytes 786440 | tf_op jit(solution)/shard_map/ppermute | solution.py:615
  128.7 4.9 %copy-start.4 = (bf16[32,32,128]{2,1,0:T(8,128)(2,1)}, bf16[32,32,128]{2,1,0:T(8,128)(2,1)S(1)}, u32[]{:S(2)}) copy-start(bf16[32,32,128]{2,1,0:T(8,128)(2,1)S(1)} %collective-permute-done.refs_1_) | copy-start | bytes 786436
  128.7 4.9 %collective-permute-start.2 = (bf16[32,32,128]{2,1,0:T(8,128)(2,1)S(1)}, bf16[32,32,128]{2,1,0:T(8,128)(2,1)S(1)}, u32[]{:S(2)}, u32[]{:S(2)}) collective-permute-start(bf16[32,32,128]{2,1,0:T(8,128)(2,1)S(1)} %collective-permute-done.refs_1_), channel_id=1, source_target_pairs={{0,1},{1,0},{2,3},{3,2},{4,5},{5,4},{6,7},{7,6},{8,9},{9,8},{10,11... | collective-permute-start | bytes 786440 | tf_op jit(solution)/shard_map/ppermute | solution.py:615
  133.7 0.7 copy-start.5
  134.4 0.7 copy-start.6

commit v2 on v1

v2 whole, which is shorter than its diff:
```python
import functools

import jax
import jax.numpy as jnp
from jax import lax
from jax.experimental import pallas as pl
from jax.experimental.pallas import tpu as pltpu
from jax.sharding import PartitionSpec as P

ridge_term = 0.01
bf16 = jnp.bfloat16
f32 = jnp.float32
vmem = functools.partial(pl.BlockSpec, memory_space=pltpu.VMEM)
smem = functools.partial(pl.BlockSpec, memory_space=pltpu.SMEM)
mib = 1024 * 1024
trailer_rows = 8


def up(value, step):
    return -(-value // step) * step


def cost(flops, moved):
    return pl.CostEstimate(flops=flops, bytes_accessed=moved, transcendentals=0)


def route_body(src, blk, request, slot_of, sender, count, *, peers, capacity):
    def clear_count(p, carry):
        count[p] = 0
        return carry

    def clear_slot(s, carry):
        sender[s] = 0
        request[s // capacity, 0, s % capacity] = 0
        return carry

    lax.fori_loop(0, peers, clear_count, 0, unroll=peers <= 16)
    lax.fori_loop(0, peers * capacity, clear_slot, 0, unroll=peers <= 16)
    for b in range(src.shape[1]):
        owner = src[0, b]
        place = count[owner]
        count[owner] = place + 1
        slot_of[b] = owner * capacity + place
        sender[owner * capacity + place] = b
        request[owner, 0, place] = blk[0, b] + 1


def route_tables(routes_src, routes_blk, peers, capacity):
    return pl.pallas_call(
        functools.partial(route_body, peers=peers, capacity=capacity),
        out_shape=(
            jax.ShapeDtypeStruct((peers, 1, capacity), jnp.int32),
            jax.ShapeDtypeStruct((routes_src.shape[1],), jnp.int32),
            jax.ShapeDtypeStruct((peers * capacity,), jnp.int32),
        ),
        in_specs=[smem()] * 2,
        out_specs=(smem(), smem(), smem()),
        scratch_shapes=[pltpu.SMEM((peers,), jnp.int32)],
        name="route_tables",
    )(routes_src, routes_blk)


def pick_body(incoming, template, out, *, capacity):
    def one(s, carry):
        block = jnp.maximum(incoming[s // capacity, 0, s % capacity] - 1, 0)
        out[s] = template[block]
        return carry

    lax.fori_loop(0, out.shape[0], one, 0, unroll=True if out.shape[0] <= 32 else 4)


def pick_blocks(incoming, template, slots, capacity):
    return pl.pallas_call(
        functools.partial(pick_body, capacity=capacity),
        out_shape=jax.ShapeDtypeStruct((slots,) + template.shape[1:], template.dtype),
        in_specs=[smem(), vmem()],
        out_specs=vmem(),
        compiler_params=pltpu.CompilerParams(vmem_limit_bytes=16 * mib),
        name="pick_blocks",
    )(incoming, template)


def store_parts(sender, image, out, side, exps, capacity, across_blocks):
    part = side // exps
    slots = sender.shape[0]

    def one(s, carry):
        b = sender[s]
        top = pl.multiple_of((b // across_blocks) * side, side)
        left = pl.multiple_of((b % across_blocks) * side, side)
        block = image[pl.ds(top, side), pl.ds(left, side)].astype(bf16)
        row = pl.multiple_of((s % capacity) * part, part)
        for q in range(exps):
            out[(s // capacity) * exps + q, pl.ds(row, part), :] = block[q * part : (q + 1) * part]
        return carry

    lax.fori_loop(0, slots, one, 0, unroll=True if slots <= 32 else 4)


def send_body(sender, request, image, out, *, side, exps, capacity, across_blocks):
    store_parts(sender, image, out, side, exps, capacity, across_blocks)
    part = side // exps
    lane = lax.broadcasted_iota(jnp.int32, (trailer_rows, side), 1)

    def put(p, carry):
        line = jnp.zeros((trailer_rows, side), f32)
        for c in range(capacity):
            line = jnp.where(lane == c, request[p, 0, c].astype(f32), line)
        for q in range(exps):
            out[p * exps + q, capacity * part :, :] = line.astype(bf16)
        return carry

    lax.fori_loop(0, request.shape[0], put, 0)


def send_parts(sender, request, image, side, exps, capacity):
    part = side // exps
    peers = request.shape[0]
    body = functools.partial(
        send_body, side=side, exps=exps, capacity=capacity, across_blocks=image.shape[1] // side
    )
    return pl.pallas_call(
        body,
        out_shape=jax.ShapeDtypeStruct(
            (peers * exps, capacity * part + trailer_rows, side), bf16
        ),
        in_specs=[smem(), smem(), vmem()],
        out_specs=vmem(),
        compiler_params=pltpu.CompilerParams(vmem_limit_bytes=16 * mib),
        name="send_parts",
    )(sender, request, image)


def cut(ref, top, left, height, side):
    down = pl.multiple_of((top // 8) * 8, 8)
    over = pl.multiple_of((left // side) * side, side)
    tile = ref[pl.ds(down, height), pl.ds(over, 3 * side)]
    tile = pltpu.roll(tile, lax.rem(3 * side - (left - over), 3 * side), 1)[:, : 2 * side]
    return pltpu.roll(tile, lax.rem(height - (top - down), height), 0)


def prepare_body(
    rows_at, cols_at, science, variance, col, rev, col_out, row_out, root_out, data_out, image, var
):
    side = rev.shape[1]
    high, wide = science.shape
    sub = lax.broadcasted_iota(jnp.int32, (side, side), 0)
    lane = lax.broadcasted_iota(jnp.int32, (side, side), 1)
    for k in range(row_out.shape[0]):
        line = jnp.broadcast_to(col[k : k + 1, :], (side, side))
        line = pltpu.roll(line, 0, 1, stride=1, stride_axis=0)
        rows = slice(k * side, (k + 1) * side)
        col_out[rows, :side] = jnp.where(lane >= sub, line, 0.0).astype(bf16)
        col_out[rows, side:] = jnp.where(lane < sub, line, 0.0).astype(bf16)
        line = jnp.broadcast_to(rev[k : k + 1, :], (side, side))
        line = pltpu.roll(line, 0, 1, stride=1, stride_axis=0)
        row_out[k, :side, :] = jnp.where(lane <= sub, line, 0.0).astype(bf16)
        row_out[k, side:, :] = jnp.where(lane > sub, line, 0.0).astype(bf16)
    image[:, wide:] = jnp.zeros((image.shape[0], image.shape[1] - wide), f32)
    image[high:, :wide] = jnp.zeros((image.shape[0] - high, wide), f32)
    image[:high, :wide] = science[...].astype(f32)
    var[:, wide:] = jnp.ones((var.shape[0], var.shape[1] - wide), f32)
    var[high:, :wide] = jnp.ones((var.shape[0] - high, wide), f32)
    var[:high, :wide] = variance[...].astype(f32)
    for s in range(rows_at.shape[1]):
        top = rows_at[0, s]
        left = cols_at[0, s]
        root = lax.rsqrt(cut(var, top, left, side + 8, side)[:side, :side])
        root_out[s * side : (s + 1) * side, :] = root
        data = cut(image, top, left, side + 8, side)[:side, :side]
        data_out[s * side : (s + 1) * side, :] = data * root


def prepare(rows_at, cols_at, science, variance, col, rev, count):
    side = rev.shape[1]
    high, wide = science.shape
    stamps = rows_at.shape[1]
    return pl.pallas_call(
        prepare_body,
        out_shape=(
            jax.ShapeDtypeStruct((count * side, 2 * side), bf16),
            jax.ShapeDtypeStruct((count, 2 * side, side), bf16),
            jax.ShapeDtypeStruct((stamps * side, side), f32),
            jax.ShapeDtypeStruct((stamps * side, side), f32),
        ),
        in_specs=[smem()] * 2 + [vmem()] * 4,
        out_specs=(vmem(),) * 4,
        scratch_shapes=[pltpu.VMEM((high + 8, wide + 2 * side), f32)] * 2,
        compiler_params=pltpu.CompilerParams(vmem_limit_bytes=24 * mib),
        name="prepare",
    )(rows_at, cols_at, science, variance, col, rev)


def normal_body(
    slot_of,
    rows_at,
    cols_at,
    arrived,
    col_bands,
    row_bands,
    roots,
    data,
    gram_out,
    windows,
    frame,
    vert,
    design,
    *,
    across_blocks,
    taps,
):
    count, _, side = row_bands.shape
    margin = taps // 2
    stamps = rows_at.shape[1]
    span = up(side + taps - 1, 16)
    padded_k = gram_out.shape[1]
    lines_all = stamps * side

    frame[...] = jnp.zeros(frame.shape, f32)
    for b in range(slot_of.shape[0]):
        top = margin + (b // across_blocks) * side
        left = margin + (b % across_blocks) * side
        frame[top : top + side, left : left + side] = arrived[slot_of[b]].astype(f32)

    cuts = []
    for s in range(stamps):
        cuts.append(cut(frame, rows_at[0, s], cols_at[0, s], span, side).astype(bf16))
    design[pl.ds(count, lines_all, stride=padded_k), :] = roots[...]
    design[pl.ds(count + 1, lines_all, stride=padded_k), :] = data[...]
    for extra in range(count + 2, padded_k):
        design[pl.ds(extra, lines_all, stride=padded_k), :] = jnp.zeros((lines_all, side), f32)

    group = vert.shape[0]
    for k in range(0, count, group):
        filters = col_bands[k * side : (k + group) * side, :span]
        for s in range(stamps):
            out = jnp.dot(filters, cuts[s], preferred_element_type=f32).astype(bf16)
            for a in range(group):
                vert[a, s * side : (s + 1) * side, :] = out[a * side : (a + 1) * side]
        for a in range(group):
            out = jnp.dot(vert[a], row_bands[k + a], preferred_element_type=f32)
            design[pl.ds(k + a, lines_all, stride=padded_k), :] = out * roots[...]

    lines = 16

    def gram_step(step, total):
        start = pl.multiple_of(step * lines * padded_k, lines * padded_k)
        rows = design[pl.ds(start, lines * padded_k), :]
        tops = []
        lows = []
        for j in range(lines):
            line = rows[j * padded_k : (j + 1) * padded_k]
            top = line.astype(bf16)
            tops.append(top)
            lows.append((line - top.astype(f32)).astype(bf16))
        tops = jnp.concatenate(tops, axis=1)
        both = jnp.concatenate([tops, jnp.concatenate(lows, axis=1)], axis=0)
        return total + lax.dot_general(
            both, tops, (((1,), (1,)), ((), ())), preferred_element_type=f32
        )

    gram_out[...] = lax.fori_loop(
        0, lines_all // lines, gram_step, jnp.zeros((2 * padded_k, padded_k), f32)
    )
    step = side - taps + 1
    for c in range(windows.shape[0]):
        windows[c] = frame[:, c * step : c * step + side]


def normal_matrix(
    slot_of, rows_at, cols_at, arrived, col_bands, row_bands, roots, data, high, wide, taps
):
    count, _, side = row_bands.shape
    stamps = rows_at.shape[1]
    padded_k = up(count + 2, 16)
    pairs = (taps + 2) // 2
    tall = up(high - side + 8 + up(side + taps - 1, 16), 16)
    tall = max(tall, up(high + 2 * pairs, 16))
    wins = -(-wide // (side - taps + 1))
    group = next(g for g in (4, 2, 1) if count % g == 0)
    return pl.pallas_call(
        functools.partial(normal_body, across_blocks=wide // side, taps=taps),
        out_shape=(
            jax.ShapeDtypeStruct((2 * padded_k, padded_k), f32),
            jax.ShapeDtypeStruct((wins, tall, side), f32),
        ),
        in_specs=[smem()] * 3 + [vmem()] * 5,
        out_specs=(vmem(),) * 2,
        scratch_shapes=[
            pltpu.VMEM((tall, wide + 2 * side), f32),
            pltpu.VMEM((group, stamps * side, 2 * side), bf16),
            pltpu.VMEM((stamps * side * padded_k, side), f32),
        ],
        compiler_params=pltpu.CompilerParams(vmem_limit_bytes=36 * mib),
        cost_estimate=cost(10_000_000_000, 8_000_000),
        name="normal_matrix",
    )(slot_of, rows_at, cols_at, arrived, col_bands, row_bands, roots, data)


def subtract_body(
    sender,
    gram,
    frames,
    science,
    col_t,
    row_rev,
    coef_out,
    payload,
    diff_out,
    windows,
    image,
    bands,
    *,
    exps,
    capacity,
    count,
    taps,
    pixels,
):
    side = frames.shape[2]
    high, wide = science.shape
    padded_k = gram.shape[1]
    part = side // exps
    size = count + 1

    square = jnp.concatenate(
        [gram[...], jnp.zeros((2 * padded_k, side - padded_k), f32)], axis=1
    )
    cross = square[padded_k:]
    mirror = jnp.concatenate([cross, jnp.zeros((side - padded_k, side), f32)], axis=0).T
    system = (square[:padded_k] + cross + mirror[:padded_k]) / pixels
    sub = lax.broadcasted_iota(jnp.int32, (padded_k, side), 0)
    lane = lax.broadcasted_iota(jnp.int32, (padded_k, side), 1)
    system = jnp.where((sub < size) & (lane <= size), system, 0.0)
    system = system + jnp.where((sub == lane) & (sub < size), ridge_term, 0.0)

    for k in range(size):
        row = system[k : k + 1, :]
        factor = system[:, k : k + 1] * (1.0 / row[:, k : k + 1])
        factor = jnp.where(sub[:, :1] == k, 0.0, factor)
        system = system - factor * row
    pivot = jnp.sum(jnp.where(sub == lane, system, 0.0), axis=1, keepdims=True)
    solved = system[:, size : size + 1] / jnp.where(sub[:, :1] < size, pivot, 1.0)
    coef_out[...] = jnp.sum(jnp.where(sub == lane, solved, 0.0), axis=0, keepdims=True)
    background = solved[count : count + 1, :]
    basis_coef = jnp.where(sub[:, :1] < count, solved, 0.0)

    scaled = basis_coef * row_rev[...]
    kernel = jnp.zeros((col_t.shape[0], side), f32)
    for _ in range(3):
        piece = scaled.astype(bf16)
        scaled = scaled - piece.astype(f32)
        kernel = kernel + jnp.dot(col_t[...], piece, preferred_element_type=f32)
    kernel_sum = jnp.sum(jnp.sum(kernel, axis=1, keepdims=True), axis=0, keepdims=True)
    rounded = kernel.astype(bf16).astype(f32)

    zero_band = jnp.zeros((side, side), bf16)

    def band(i):
        if i < 0 or i >= taps:
            return zero_band
        line = jnp.broadcast_to(rounded[i : i + 1, :], (side, side))
        return pltpu.roll(line, 0, 1, stride=1, stride_axis=0).astype(bf16)

    pairs = (taps + 2) // 2
    made = {i: band(i) for i in range(-1, 2 * pairs)}
    for q in range(pairs):
        for a in range(2):
            for b in range(2):
                bands[
                    q * 2 * side + a * side : q * 2 * side + (a + 1) * side,
                    b * side : (b + 1) * side,
                ] = made[2 * q + a - b]

    step = side - taps + 1
    rows_half = high // 2
    for c in range(windows.shape[0]):
        lhs = jnp.concatenate(
            [
                frames[c, pl.ds(row, rows_half, stride=2), :].astype(bf16)
                for row in range(2 * pairs)
            ],
            axis=1,
        )
        out = jnp.dot(lhs, bands[...], preferred_element_type=f32)
        windows[c, pl.ds(0, rows_half, stride=2), :] = out[:, :side]
        windows[c, pl.ds(1, rows_half, stride=2), :] = out[:, side:]
        keep = min(step, wide - c * step)
        image[:, c * step : c * step + keep] = windows[c, :, :keep]
    diff_out[...] = (science[...].astype(f32) - image[...] - background).astype(bf16)

    store_parts(sender, diff_out, payload, side, exps, capacity, wide // side)
    line_at = lax.broadcasted_iota(jnp.int32, (trailer_rows, side), 0)
    trailer = jnp.zeros((trailer_rows, side), f32)
    rest = kernel_sum
    for p in range(3):
        piece = rest.astype(bf16).astype(f32)
        rest = rest - piece
        trailer = jnp.where(line_at == p, piece, trailer)
    trailer = trailer.astype(bf16)

    def put(d, carry):
        payload[d, capacity * part :, :] = trailer
        return carry

    lax.fori_loop(0, payload.shape[0], put, 0, unroll=4)


def subtract(
    sender, gram, frames, science, col_t, row_rev, peers, exps, capacity, count, taps, pixels
):
    wins, _, side = frames.shape
    high, wide = science.shape
    part = side // exps
    pairs = (taps + 2) // 2
    body = functools.partial(
        subtract_body, exps=exps, capacity=capacity, count=count, taps=taps, pixels=pixels
    )
    return pl.pallas_call(
        body,
        out_shape=(
            jax.ShapeDtypeStruct((1, side), f32),
            jax.ShapeDtypeStruct(
                (peers * exps, capacity * part + trailer_rows, side), bf16
            ),
            jax.ShapeDtypeStruct((high, wide), bf16),
        ),
        in_specs=[smem()] + [vmem()] * 5,
        out_specs=(vmem(), vmem(), vmem()),
        scratch_shapes=[
            pltpu.VMEM((wins, high, side), f32),
            pltpu.VMEM((high, wide), f32),
            pltpu.VMEM((pairs * 2 * side, 2 * side), bf16),
        ],
        compiler_params=pltpu.CompilerParams(vmem_limit_bytes=24 * mib),
        cost_estimate=cost(5_000_000_000, 4_000_000),
        name="subtract",
    )(sender, gram, frames, science, col_t, row_rev)


def split2(value):
    top = value.astype(bf16)
    return top, (value - top.astype(f32)).astype(bf16)


def psf_body(diff, down, over, out, padded, sideways, *, side, taps):
    high, wide = diff.shape
    margin = taps // 2
    span = up(side + taps - 1, 16)
    padded[...] = jnp.zeros(padded.shape, f32)
    padded[:, margin : margin + wide] = diff[...].astype(f32)
    line = jnp.broadcast_to(over[...], (2 * side, 2 * side))
    band = pltpu.roll(line, 0, 1, stride=1, stride_axis=0)[:, :side]
    both = jnp.concatenate(split2(band), axis=1)
    sideways[...] = jnp.zeros(sideways.shape, f32)
    for c in range(wide // side):
        window = padded[:, c * side : (c + 2) * side].astype(bf16)
        got = jnp.dot(window, both, preferred_element_type=f32)
        sideways[margin : margin + high, c * side : (c + 1) * side] = got[:, :side] + got[:, side:]
    line = jnp.broadcast_to(down[...], (side, 2 * side))
    band = pltpu.roll(line, 0, 1, stride=1, stride_axis=0)[:, :span]
    top, low = split2(band)
    for r in range(high // side):
        data_top, data_low = split2(sideways[r * side : r * side + span, :])
        got = jnp.dot(top, data_top, preferred_element_type=f32)
        got = got + jnp.dot(top, data_low, preferred_element_type=f32)
        got = got + jnp.dot(low, data_top, preferred_element_type=f32)
        out[r * side : (r + 1) * side, :] = got


def correlate(diff, down, over_rev, side, taps):
    high, wide = diff.shape
    span = up(side + taps - 1, 16)
    return pl.pallas_call(
        functools.partial(psf_body, side=side, taps=taps),
        out_shape=jax.ShapeDtypeStruct((high, wide), f32),
        in_specs=[vmem()] * 3,
        out_specs=vmem(),
        scratch_shapes=[
            pltpu.VMEM((high, wide + side), f32),
            pltpu.VMEM((high - side + span, wide), f32),
        ],
        compiler_params=pltpu.CompilerParams(vmem_limit_bytes=16 * mib),
        cost_estimate=cost(2_000_000_000, 2_000_000),
        name="correlate",
    )(diff, down, over_rev)


def variance_body(table, parts, out, total, *, part, capacity):
    total[...] = jnp.zeros(total.shape, f32)
    tract = out.shape[0]

    def one(j, carry):
        block = table[j // capacity, j % capacity] - 1
        block = jnp.where(block < 0, tract, block)
        row = pl.multiple_of((j % capacity) * part, part)
        total[block] += parts[j // capacity, pl.ds(row, part), :].astype(f32)
        return carry

    lax.fori_loop(0, parts.shape[0] * capacity, one, 0, unroll=8)
    out[...] = total[:tract]


def sum_variance(table, parts, tract, part, capacity):
    side = parts.shape[2]
    return pl.pallas_call(
        functools.partial(variance_body, part=part, capacity=capacity),
        out_shape=jax.ShapeDtypeStruct((tract, part, side), f32),
        in_specs=[smem(), vmem()],
        out_specs=vmem(),
        scratch_shapes=[pltpu.VMEM((tract + 1, part, side), f32)],
        compiler_params=pltpu.CompilerParams(vmem_limit_bytes=16 * mib),
        name="sum_variance",
    )(table, parts)


def combine_body(table, parts, var_sum, var_template, out, total, gain, *, part, capacity):
    total[...] = jnp.zeros(total.shape, f32)
    gain[...] = jnp.zeros(gain.shape, f32)
    tract = out.shape[0]

    def one(d, carry):
        tail = parts[d, capacity * part :, :].astype(f32)
        kernel_sum = tail[0:1] + tail[1:2] + tail[2:3]
        square = jnp.broadcast_to(kernel_sum * kernel_sum, gain.shape[1:])
        for c in range(capacity):
            block = table[d, c] - 1
            block = jnp.where(block < 0, tract, block)
            total[block] += parts[d, c * part : (c + 1) * part, :].astype(f32)
            gain[block] += square
        return carry

    lax.fori_loop(0, parts.shape[0], one, 0, unroll=4)
    for t in range(tract):
        variance = var_sum[t] + gain[t, 0:1, :] * var_template[t].astype(f32)
        out[t] = (total[t] * lax.rsqrt(jnp.maximum(variance, 1.0))).astype(bf16)


def combine(table, parts, var_sum, var_template, part, capacity):
    tract, _, side = var_sum.shape
    return pl.pallas_call(
        functools.partial(combine_body, part=part, capacity=capacity),
        out_shape=jax.ShapeDtypeStruct((tract, part, side), bf16),
        in_specs=[smem(), vmem(), vmem(), vmem()],
        out_specs=vmem(),
        scratch_shapes=[
            pltpu.VMEM((tract + 1, part, side), f32),
            pltpu.VMEM((tract + 1, 8, side), f32),
        ],
        compiler_params=pltpu.CompilerParams(vmem_limit_bytes=16 * mib),
        name="combine",
    )(table, parts, var_sum, var_template)


def join_body(places, *refs, part, chunk):
    out, held, sems = refs[-3:]
    copies = []
    for i in range(out.shape[0] // chunk):
        blocks = pl.ds(i * chunk, chunk)
        for d, ref in enumerate(refs[:-3]):
            row = pl.multiple_of(places[d] * part, part)
            held[blocks, pl.ds(row, part), :] = ref[blocks].astype(f32)
        copies.append(pltpu.make_async_copy(held.at[blocks], out.at[blocks], sems.at[i]))
        copies[-1].start()
    for copy in copies:
        copy.wait()


def join_parts(places, parts):
    tract, part, side = parts[0].shape
    exps = len(parts)
    chunk = 8 if tract % 8 == 0 else tract
    return pl.pallas_call(
        functools.partial(join_body, part=part, chunk=chunk),
        out_shape=jax.ShapeDtypeStruct((tract, part * exps, side), f32),
        in_specs=[smem()] + [vmem()] * exps,
        out_specs=pl.BlockSpec(memory_space=pl.ANY),
        scratch_shapes=[
            pltpu.VMEM((tract, part * exps, side), f32),
            pltpu.SemaphoreType.DMA((tract // chunk,)),
        ],
        compiler_params=pltpu.CompilerParams(vmem_limit_bytes=16 * mib),
        name="join_parts",
    )(places, *parts)


def local(
    template,
    template_var,
    science,
    science_var,
    routes_src,
    routes_blk,
    stamp_rows,
    stamp_cols,
    basis_col,
    basis_row,
    psf_col,
    psf_row,
):
    peers = lax.axis_size("det")
    exps = lax.axis_size("exp")
    me = lax.axis_index("exp").astype(jnp.int32)
    tract, side, _ = template.shape
    science_img = science[0]
    variance_img = science_var[0]
    blocks_dev = routes_src.shape[1]
    count, taps = basis_col.shape
    capacity = max(2, -(-blocks_dev // peers))
    slots = peers * capacity
    part = side // exps

    request, slot_of, sender = route_tables(routes_src, routes_blk, peers, capacity)
    incoming = lax.all_to_all(request, "det", split_axis=0, concat_axis=0, tiled=True)
    picked = pick_blocks(incoming, template, slots, capacity)
    arrived = lax.all_to_all(picked, "det", split_axis=0, concat_axis=0, tiled=True)

    padded_k = up(count + 2, 16)
    col_t = jnp.pad(basis_col.T, ((0, up(taps, 16) - taps), (0, padded_k - count)))
    col = jnp.pad(basis_col.astype(f32), ((0, padded_k - count), (0, side - taps)))
    row_rev = jnp.pad(
        basis_row.astype(f32)[:, ::-1], ((0, padded_k - count), (side - taps, 0))
    )
    row_rev = jnp.roll(row_rev, 1, axis=1)
    over_rev = jnp.roll(jnp.pad(psf_row[:, ::-1], ((0, 0), (2 * side - taps, 0))), 1, axis=1)
    down = jnp.pad(psf_col, ((0, 0), (0, 2 * side - taps)))
    col_bands, row_bands, roots, data = prepare(
        stamp_rows, stamp_cols, science_img, variance_img, col, row_rev, count
    )
    sender_late, col_bands, row_bands, col_t, over_rev, down = lax.optimization_barrier(
        (sender, col_bands, row_bands, col_t, over_rev, down)
    )
    var_parts = send_parts(sender_late, request, variance_img, side, exps, capacity)
    var_back = lax.all_to_all(
        var_parts, ("det", "exp"), split_axis=0, concat_axis=0, tiled=True
    )
    table = var_back[:, capacity * part, :capacity].astype(f32).astype(jnp.int32)

    gram, frames = normal_matrix(
        slot_of,
        stamp_rows,
        stamp_cols,
        arrived,
        col_bands,
        row_bands,
        roots,
        data,
        science_img.shape[0],
        science_img.shape[1],
        taps,
    )
    coef, payload, difference = subtract(
        sender,
        gram,
        frames,
        science_img,
        col_t,
        row_rev,
        peers,
        exps,
        capacity,
        count,
        taps,
        stamp_rows.shape[1] * side * side,
    )
    diff_back = lax.all_to_all(payload, ("det", "exp"), split_axis=0, concat_axis=0, tiled=True)
    scored = correlate(difference, down, over_rev, side, taps)
    var_sum = sum_variance(table, var_back, tract, part, capacity)
    var_template = lax.dynamic_slice_in_dim(template_var, me * part, part, 1)
    var_sum, scored = lax.optimization_barrier((var_sum, scored))
    mine = combine(table, diff_back, var_sum, var_template, part, capacity)

    if exps & (exps - 1) == 0:
        held = [mine]
        reach = exps // 2
        gaps = [0]
        while reach:
            pairs = [(e, e ^ reach) for e in range(exps)]
            held = held + [lax.ppermute(h, "exp", pairs) for h in held]
            gaps = gaps + [g ^ reach for g in gaps]
            reach //= 2
        places = jnp.stack([me ^ g for g in gaps])
    else:
        held = [mine]
        for gap in range(1, exps):
            pairs = [(e, (e + gap) % exps) for e in range(exps)]
            held.append(lax.ppermute(mine, "exp", pairs))
        places = jnp.stack([(me - g) % exps for g in range(exps)])
    significance = join_parts(places, held)
    return (significance, scored[None], coef[:, : count + 1])


def solution(mesh):
    placed = (
        P("det", None, None),
        P("det", None, None),
        P("exp", "det", None),
        P("exp", "det", None),
        P("exp", "det"),
        P("exp", "det"),
        P("exp", "det"),
        P("exp", "det"),
        P(),
        P(),
        P("exp", None),
        P("exp", None),
    )
    return jax.shard_map(
        local,
        mesh=mesh,
        in_specs=placed,
        out_specs=(P("det", None, None), P("exp", "det", None), P("exp", "det")),
        check_vma=False,
    )
```

time: 140 us -> 105 us (0.75)
  Pallas kernels: 64.8 us -> 39.7 us
  blocking collectives: 0 us -> 11.6 us
  waiting for transfers between devices: 32.9 us -> 22.6 us
  local copies, waits for them, and re-layouts: 13.4 us -> 8.44 us
  starting transfers between devices: 23.8 us -> 20.5 us
  other arithmetic: 1.93 us -> 0.28 us
  matrix products: 1.58 us -> 0 us
    pallas_call x4 -> x6, Pallas kernels: 52.4 us -> 33.2 us  [the longest x1 18.1 us: normal_matrix(): pl.pallas_call(functools.partial(normal_body, across_blocks=wide // side,...]
    all_to_all x0 -> x1, blocking collectives: none -> 11.6 us  [local(): lax.all_to_all(request, 'det', split_axis=0, concat_axis=0, tiled=True)]
    all_to_all x1 -> x0, starting transfers between devices: 7.1 us -> none  [local(): lax.all_to_all(request, ('det', 'exp'), split_axis=0, concat_axis=0, tile...]
    all_to_all x1 -> x0, waiting for transfers between devices: 6.69 us -> none  [local(): lax.all_to_all(request, ('det', 'exp'), split_axis=0, concat_axis=0, tile...]
    all_to_all x1, waiting for transfers between devices: 8.25 us -> 3.05 us  [local(): lax.all_to_all(picked, 'det', split_axis=0, concat_axis=0, tiled=True)]
    convert_element_type x1 -> x0, local copies, waits for them, and re-layouts: 5.09 us -> none  [local(): col_bands = col_bands.astype(bf16).reshape(count * side, span)]
    unnamed x22 -> x35, local copies, waits for them, and re-layouts: 3.05 us -> 7.91 us
    all_to_all x1, starting transfers between devices: 4.26 us -> 7.89 us  [local(): lax.all_to_all(var_parts, ('det', 'exp'), split_axis=0, concat_axis=0, ti...]
  transfers between devices with their start and end apart: 7 -> 6, of which waited for: 4 -> 4; matrix products, arithmetic and copies ran while one was open for 9% -> 1% of each run, Pallas kernels for 26% -> 32%
where the time goes in v2:
time: 105 us; the launch traced here: 104 us
  Pallas kernels  39.7 us (38%)
  waiting for transfers between devices  22.6 us (22%)
  starting transfers between devices  20.5 us (20%)
  blocking collectives  11.6 us (11%)
  local copies, waits for them, and re-layouts  8.44 us (8%)
    pallas_call x1, Pallas kernels, normal_matrix(): pl.pallas_call(functools.partial(normal_body, across_blocks=wide // side,...  18.1 us
    all_to_all x1, waiting for transfers between devices, local(): lax.all_to_all(payload, ('det', 'exp'), split_axis=0, concat_axis=0, tile...  12.8 us
    all_to_all x1, blocking collectives, local(): lax.all_to_all(request, 'det', split_axis=0, concat_axis=0, tiled=True)  11.6 us
    pallas_call x1, Pallas kernels, subtract(): pl.pallas_call(body, out_shape=(jax.ShapeDtypeStruct((1, side), f32), jax...  7.99 us
    unnamed x35, local copies, waits for them, and re-layouts  7.91 us
    all_to_all x1, starting transfers between devices, local(): lax.all_to_all(var_parts, ('det', 'exp'), split_axis=0, concat_axis=0, ti...  7.89 us
    ppermute x3, waiting for transfers between devices, local(): held = held + [lax.ppermute(h, 'exp', pairs) for h in held]  6.74 us
    all_to_all x1, starting transfers between devices, local(): lax.all_to_all(payload, ('det', 'exp'), split_axis=0, concat_axis=0, tile...  5.82 us
  transfers between devices with their start and end apart: 6, of which 4 were waited for; matrix products, arithmetic and copies ran while one was open for 1% of the time, Pallas kernels for 32%

profile of v2, /device:TPU:1, one launch (start us, length us, event | category | flops | bytes accessed | tf_op | source)
XLA Modules:
  0.0 104.2 jit_solution(16376332303428543992)
XLA Ops:
  0.7 1.5 %route_tables.1 = (s32[8,1,2]{2,1,0:T(1,128)}, s32[16]{0:T(128)}, s32[16]{0:T(128)}) custom-call(s32[1,16]{1,0:T(1,128)} %src.1, s32[1,16]{1,0:T(1,128)} %blk.1), custom_call_target="tpu_custom_call" | custom-call | tf_op jit(solution)/shard_map/route_tables/pallas_call | solution.py:49
  2.2 11.6 %all_to_all.20.incoming = s32[8,1,2]{2,1,0:T(1,128)S(1)} all-to-all(s32[8,1,2]{2,1,0:T(1,128)} %get-tuple-element.27.request), channel_id=1, replica_groups=mesh['det'=8,'exp'=4] {'det'}, dimensions={0} | all-to-all | bytes 128 | tf_op jit(solution)/shard_map/all_to_all | solution.py:614
  13.8 1.2 %copy-done.2 = bf16[32,128,128]{2,1,0:T(8,128)(2,1)S(1)} copy-done((bf16[32,128,128]{2,1,0:T(8,128)(2,1)S(1)}, bf16[32,128,128]{2,1,0:T(8,128)(2,1)}, u32[]{:S(2)}) %copy-start.2) | copy-done | bytes 1048600
  15.1 1.4 %pick_blocks.1 = bf16[16,128,128]{2,1,0:T(8,128)(2,1)} custom-call(s32[8,1,2]{2,1,0:T(1,128)S(1)} %all_to_all.20.incoming, bf16[32,128,128]{2,1,0:T(8,128)(2,1)S(1)} %copy-done.2), custom_call_target="tpu_custom_call" | custom-call | tf_op jit(solution)/shard_map/pick_blocks/pallas_call | solution.py:73
  16.5 3.6 %all-to-all-start.2 = ((bf16[16,128,128]{2,1,0:T(8,128)(2,1)}), bf16[16,128,128]{2,1,0:T(8,128)(2,1)S(1)}, u32[]{:S(2)}, u32[]{:S(2)}) async-start(bf16[16,128,128]{2,1,0:T(8,128)(2,1)} %pick_blocks.1), calls=%async_computation.2 | async-start | bytes 1048576 | tf_op jit(solution)/shard_map/all_to_all | solution.py:616
  20.8 2.3 %prepare.1 = (bf16[5120,256]{1,0:T(8,128)(2,1)S(1)}, bf16[40,256,128]{2,1,0:T(8,128)(2,1)S(1)}, f32[512,128]{1,0:T(8,128)S(1)}, f32[512,128]{1,0:T(8,128)S(1)}) custom-call(s32[1,4]{1,0:T(1,128)S(1)} %copy-done.5, s32[1,4]{1,0:T(1,128)S(1)} %copy-done.6, bf16[256,1024]{1,0:T(8,128)(2,1)S(1)} %bitcast.13, bf16[256,1024]{1,0:T(8,128)(2,1)S(1)} %bitcast.11, ...), custom_call_target="tpu_custom_call" | custom-call | tf_op jit(solution)/shard_map/prepare/pallas_call | solution.py:178
  23.2 1.5 %copy-done.8 = bf16[5120,256]{1,0:T(8,128)(2,1)} copy-done((bf16[5120,256]{1,0:T(8,128)(2,1)}, bf16[5120,256]{1,0:T(8,128)(2,1)S(1)}, u32[]{:S(2)}) %copy-start.8) | copy-done | bytes 2621464
  24.7 1.5 %copy-done.10 = bf16[40,256,128]{2,1,0:T(8,128)(2,1)} copy-done((bf16[40,256,128]{2,1,0:T(8,128)(2,1)}, bf16[40,256,128]{2,1,0:T(8,128)(2,1)S(1)}, u32[]{:S(2)}) %copy-start.10) | copy-done | bytes 2621464
  26.4 1.6 %send_parts.1 = bf16[32,72,128]{2,1,0:T(8,128)(2,1)} custom-call(s32[16]{0:T(128)S(1)} %copy-done.7, s32[8,1,2]{2,1,0:T(1,128)S(1)} %copy-done.4, bf16[256,1024]{1,0:T(8,128)(2,1)S(1)} %bitcast.12), custom_call_target="tpu_custom_call" | custom-call | tf_op jit(solution)/shard_map/send_parts/pallas_call | solution.py:122
  28.0 3.1 %all-to-all-done.2.arrived = bf16[16,128,128]{2,1,0:T(8,128)(2,1)S(1)} async-done(((bf16[16,128,128]{2,1,0:T(8,128)(2,1)}), bf16[16,128,128]{2,1,0:T(8,128)(2,1)S(1)}, u32[]{:S(2)}, u32[]{:S(2)}) %all-to-all-start.2) | async-done | bytes 524320 | tf_op jit(solution)/shard_map/all_to_all | solution.py:616
  31.1 7.9 %all-to-all-start = ((bf16[32,72,128]{2,1,0:T(8,128)(2,1)}), bf16[32,72,128]{2,1,0:T(8,128)(2,1)S(1)}, u32[]{:S(2)}, u32[]{:S(2)}) async-start(bf16[32,72,128]{2,1,0:T(8,128)(2,1)} %send_parts.1), calls=%async_computation | async-start | bytes 1179648 | tf_op jit(solution)/shard_map/all_to_all | solution.py:634
  39.0 1.7 %copy-done.9 = bf16[5120,256]{1,0:T(8,128)(2,1)S(1)} copy-done((bf16[5120,256]{1,0:T(8,128)(2,1)S(1)}, bf16[5120,256]{1,0:T(8,128)(2,1)}, u32[]{:S(2)}) %copy-start.9) | copy-done | bytes 2621464
  40.7 1.7 %copy-done.11 = bf16[40,256,128]{2,1,0:T(8,128)(2,1)S(1)} copy-done((bf16[40,256,128]{2,1,0:T(8,128)(2,1)S(1)}, bf16[40,256,128]{2,1,0:T(8,128)(2,1)}, u32[]{:S(2)}) %copy-start.11) | copy-done | bytes 2621464
  42.5 18.1 %normal_matrix.1 = (f32[96,48]{1,0:T(8,128)S(1)}, f32[10,304,128]{2,1,0:T(8,128)S(1)}) custom-call(s32[16]{0:T(128)S(1)} %copy-done.12, s32[1,4]{1,0:T(1,128)S(1)} %copy-done.5, s32[1,4]{1,0:T(1,128)S(1)} %copy-done.6, bf16[16,128,128]{2,1,0:T(8,128)(2,1)S(1)} %all-to-all-done.2.arrived, bf16[5120,256]{1,0:T(8,128)(2,1)S(1)} %copy-done.9, ...), custom_call_target="tpu_custom_call" | custom-call | flops 10000000000 | bytes 8000000 | tf_op jit(solution)/shard_map/normal_matrix/pallas_call | solution.py:281
  60.6 8.0 %subtract.1 = (f32[1,128]{1,0:T(1,128)}, bf16[32,72,128]{2,1,0:T(8,128)(2,1)}, bf16[256,1024]{1,0:T(8,128)(2,1)S(1)}) custom-call(s32[16]{0:T(128)S(1)} %copy-done.7, f32[96,48]{1,0:T(8,128)S(1)} %get-tuple-element.33.gram, f32[10,304,128]{2,1,0:T(8,128)S(1)} %get-tuple-element.34.frames, bf16[256,1024]{1,0:T(8,128)(2,1)S(1)} %bitcast.14, ...), custom_call_target="tpu_custom_call" | custom-call | flops 5000000000 | bytes 4000000 | tf_op jit(solution)/shard_map/subtract/pallas_call | solution.py:419
  68.5 5.8 %all-to-all-start.3 = ((bf16[32,72,128]{2,1,0:T(8,128)(2,1)}), bf16[32,72,128]{2,1,0:T(8,128)(2,1)S(1)}, u32[]{:S(2)}, u32[]{:S(2)}) async-start(bf16[32,72,128]{2,1,0:T(8,128)(2,1)} %get-tuple-element.36), calls=%async_computation.3 | async-start | bytes 1179648 | tf_op jit(solution)/shard_map/all_to_all | solution.py:666
  74.4 2.0 %correlate.1 = f32[256,1024]{1,0:T(8,128)} custom-call(bf16[256,1024]{1,0:T(8,128)(2,1)S(1)} %get-tuple-element.37.diff, f32[1,256]{1,0:T(1,128)S(1)} %pad.27.down, f32[1,256]{1,0:T(1,128)S(1)} %pad_maximum_fusion.1.over), custom_call_target="tpu_custom_call" | custom-call | flops 2000000000 | bytes 2000000 | tf_op jit(solution)/shard_map/correlate/pallas_call | solution.py:474
  76.4 1.5 %sum_variance.1.var_sum = f32[32,32,128]{2,1,0:T(8,128)S(1)} custom-call(s32[32,2]{1,0:T(8,128)S(1)} %bitcast.15, bf16[32,72,128]{2,1,0:T(8,128)(2,1)S(1)} %all-to-all-done.parts), custom_call_target="tpu_custom_call" | custom-call | tf_op jit(solution)/shard_map/sum_variance/pallas_call | solution.py:506
  78.0 12.8 %all-to-all-done.3.parts = bf16[32,72,128]{2,1,0:T(8,128)(2,1)S(1)} async-done(((bf16[32,72,128]{2,1,0:T(8,128)(2,1)}), bf16[32,72,128]{2,1,0:T(8,128)(2,1)S(1)}, u32[]{:S(2)}, u32[]{:S(2)}) %all-to-all-start.3) | async-done | bytes 589856 | tf_op jit(solution)/shard_map/all_to_all | solution.py:666
  90.8 1.3 %combine.1.refs_0_ = bf16[32,32,128]{2,1,0:T(8,128)(2,1)S(1)} custom-call(s32[32,2]{1,0:T(8,128)S(1)} %bitcast.16, bf16[32,72,128]{2,1,0:T(8,128)(2,1)S(1)} %all-to-all-done.3.parts, f32[32,32,128]{2,1,0:T(8,128)S(1)} %sum_variance.1.var_sum, bf16[32,32,128]{2,1,0:T(8,128)(2,1)S(1)} %constant_dynamic-slice_fusion.var_template), custom_call_target="tpu_custom_call" | custom-call | tf_op jit(solution)/shard_map/combine/pallas_call | solution.py:541
  92.1 1.3 %collective-permute-start = (bf16[32,32,128]{2,1,0:T(8,128)(2,1)S(1)}, bf16[32,32,128]{2,1,0:T(8,128)(2,1)S(1)}, u32[]{:S(2)}, u32[]{:S(2)}) collective-permute-start(bf16[32,32,128]{2,1,0:T(8,128)(2,1)S(1)} %combine.1.refs_0_), channel_id=1, source_target_pairs={{0,2},{1,3},{2,0},{3,1},{4,6},{5,7},{6,4},{7,5},{8,10},{9,11},{10,... | collective-permute-start | bytes 786440 | tf_op jit(solution)/shard_map/ppermute | solution.py:679
  93.9 5.7 %collective-permute-done.refs_1_ = bf16[32,32,128]{2,1,0:T(8,128)(2,1)S(1)} collective-permute-done((bf16[32,32,128]{2,1,0:T(8,128)(2,1)S(1)}, bf16[32,32,128]{2,1,0:T(8,128)(2,1)S(1)}, u32[]{:S(2)}, u32[]{:S(2)}) %collective-permute-start) | collective-permute-done | bytes 262176 | tf_op jit(solution)/shard_map/ppermute | solution.py:679
  99.5 1.4 %collective-permute-start.2 = (bf16[32,32,128]{2,1,0:T(8,128)(2,1)S(1)}, bf16[32,32,128]{2,1,0:T(8,128)(2,1)S(1)}, u32[]{:S(2)}, u32[]{:S(2)}) collective-permute-start(bf16[32,32,128]{2,1,0:T(8,128)(2,1)S(1)} %collective-permute-done.refs_1_), channel_id=1, source_target_pairs={{0,1},{1,0},{2,3},{3,2},{4,5},{5,4},{6,7},{7,6},{8,9},{9,8},{10,11... | collective-permute-start | bytes 786440 | tf_op jit(solution)/shard_map/ppermute | solution.py:679
  102.1 1.9 %join_parts.1 = f32[32,128,128]{2,1,0:T(8,128)} custom-call(s32[4]{0:T(128)S(1)} %pad_add_fusion.places, bf16[32,32,128]{2,1,0:T(8,128)(2,1)S(1)} %combine.1.refs_0_, bf16[32,32,128]{2,1,0:T(8,128)(2,1)S(1)} %collective-permute-done.refs_1_, bf16[32,32,128]{2,1,0:T(8,128)(2,1)S(1)} %collective-permute-done.1.refs_2_, ...), custom_call_target="tpu_custom_call" | custom-call | tf_op jit(solution)/shard_map/join_parts/pallas_call | solution.py:573
  (48 shorter events, 2.5 us)
Async XLA Ops:
  0.6 73.8 %copy-start = (bf16[32,128,128]{2,1,0:T(8,128)(2,1)S(1)}, bf16[32,128,128]{2,1,0:T(8,128)(2,1)}, u32[]{:S(2)}) copy-start(bf16[32,128,128]{2,1,0:T(8,128)(2,1)} %param.13) | copy-start | bytes 3145732
  0.6 20.2 %copy-start.1 = (bf16[1,256,1024]{2,1,0:T(8,128)(2,1)S(1)}, bf16[1,256,1024]{2,1,0:T(8,128)(2,1)}, u32[]{:S(2)}) copy-start(bf16[1,256,1024]{2,1,0:T(8,128)(2,1)} %param.15) | copy-start | bytes 1572868
  13.8 1.2 %copy-start.2 = (bf16[32,128,128]{2,1,0:T(8,128)(2,1)S(1)}, bf16[32,128,128]{2,1,0:T(8,128)(2,1)}, u32[]{:S(2)}) copy-start(bf16[32,128,128]{2,1,0:T(8,128)(2,1)} %template.1) | copy-start | bytes 3145732
  15.0 5.1 %copy-start.14 = (bf16[40,21]{0,1:T(8,128)(2,1)S(1)}, bf16[40,21]{0,1:T(8,128)(2,1)}, u32[]{:S(2)}) copy-start(bf16[40,21]{0,1:T(8,128)(2,1)} %param.21) | copy-start | bytes 5044
  15.0 5.3 %copy-start.13 = (bf16[40,21]{0,1:T(8,128)(2,1)S(1)}, bf16[40,21]{0,1:T(8,128)(2,1)}, u32[]{:S(2)}) copy-start(bf16[40,21]{0,1:T(8,128)(2,1)} %param.20) | copy-start | bytes 5044
  15.0 5.4 %copy-start.15 = (f32[1,21]{1,0:T(1,128)S(1)}, f32[1,21]{1,0:T(1,128)}, u32[]{:S(2)}) copy-start(f32[1,21]{1,0:T(1,128)} %param.23) | copy-start | bytes 256
  15.0 5.5 %copy-start.16 = (f32[1,21]{1,0:T(1,128)S(1)}, f32[1,21]{1,0:T(1,128)}, u32[]{:S(2)}) copy-start(f32[1,21]{1,0:T(1,128)} %param.22) | copy-start | bytes 256
  15.0 5.8 %copy-start.3 = (bf16[1,256,1024]{2,1,0:T(8,128)(2,1)S(1)}, bf16[1,256,1024]{2,1,0:T(8,128)(2,1)}, u32[]{:S(2)}) copy-start(bf16[1,256,1024]{2,1,0:T(8,128)(2,1)} %param.14) | copy-start | bytes 1572868
  15.0 5.8 %copy-start.5 = (s32[1,4]{1,0:T(1,128)S(1)}, s32[1,4]{1,0:T(1,128)}, u32[]{:S(2)}) copy-start(s32[1,4]{1,0:T(1,128)} %rows_at.3) | copy-start | bytes 52
  15.1 5.8 %copy-start.6 = (s32[1,4]{1,0:T(1,128)S(1)}, s32[1,4]{1,0:T(1,128)}, u32[]{:S(2)}) copy-start(s32[1,4]{1,0:T(1,128)} %cols_at.3) | copy-start | bytes 52
  15.1 11.3 %copy-start.4 = (s32[8,1,2]{2,1,0:T(1,128)S(1)}, s32[8,1,2]{2,1,0:T(1,128)}, u32[]{:S(2)}) copy-start(s32[8,1,2]{2,1,0:T(1,128)} %get-tuple-element.27.request) | copy-start | bytes 196
  15.1 11.3 %copy-start.7 = (s32[16]{0:T(128)S(1)}, s32[16]{0:T(128)}, u32[]{:S(2)}) copy-start(s32[16]{0:T(128)} %get-tuple-element.26.sender) | copy-start | bytes 196
  16.5 22.5 %copy-start.12 = (s32[16]{0:T(128)S(1)}, s32[16]{0:T(128)}, u32[]{:S(2)}) copy-start(s32[16]{0:T(128)} %get-tuple-element.28.slot_of) | copy-start | bytes 196
  16.5 14.6 %all-to-all-start.2 = ((bf16[16,128,128]{2,1,0:T(8,128)(2,1)}), bf16[16,128,128]{2,1,0:T(8,128)(2,1)S(1)}, u32[]{:S(2)}, u32[]{:S(2)}) async-start(bf16[16,128,128]{2,1,0:T(8,128)(2,1)} %pick_blocks.1), calls=%async_computation.2 | async-start | bytes 1048576 | tf_op jit(solution)/shard_map/all_to_all | solution.py:616
  23.1 1.5 %copy-start.8 = (bf16[5120,256]{1,0:T(8,128)(2,1)}, bf16[5120,256]{1,0:T(8,128)(2,1)S(1)}, u32[]{:S(2)}) copy-start(bf16[5120,256]{1,0:T(8,128)(2,1)S(1)} %get-tuple-element.29.col_bands) | copy-start | bytes 7864324
  24.7 1.5 %copy-start.10 = (bf16[40,256,128]{2,1,0:T(8,128)(2,1)}, bf16[40,256,128]{2,1,0:T(8,128)(2,1)S(1)}, u32[]{:S(2)}) copy-start(bf16[40,256,128]{2,1,0:T(8,128)(2,1)S(1)} %get-tuple-element.30.row_bands) | copy-start | bytes 7864324
  31.1 37.5 %all-to-all-start = ((bf16[32,72,128]{2,1,0:T(8,128)(2,1)}), bf16[32,72,128]{2,1,0:T(8,128)(2,1)S(1)}, u32[]{:S(2)}, u32[]{:S(2)}) async-start(bf16[32,72,128]{2,1,0:T(8,128)(2,1)} %send_parts.1), calls=%async_computation | async-start | bytes 1179648 | tf_op jit(solution)/shard_map/all_to_all | solution.py:634
  39.0 1.7 %copy-start.9 = (bf16[5120,256]{1,0:T(8,128)(2,1)S(1)}, bf16[5120,256]{1,0:T(8,128)(2,1)}, u32[]{:S(2)}) copy-start(bf16[5120,256]{1,0:T(8,128)(2,1)} %copy-done.8) | copy-start | bytes 7864324
  40.7 1.7 %copy-start.11 = (bf16[40,256,128]{2,1,0:T(8,128)(2,1)S(1)}, bf16[40,256,128]{2,1,0:T(8,128)(2,1)}, u32[]{:S(2)}) copy-start(bf16[40,256,128]{2,1,0:T(8,128)(2,1)} %copy-done.10) | copy-start | bytes 7864324
  68.5 22.3 %all-to-all-start.3 = ((bf16[32,72,128]{2,1,0:T(8,128)(2,1)}), bf16[32,72,128]{2,1,0:T(8,128)(2,1)S(1)}, u32[]{:S(2)}, u32[]{:S(2)}) async-start(bf16[32,72,128]{2,1,0:T(8,128)(2,1)} %get-tuple-element.36), calls=%async_computation.3 | async-start | bytes 1179648 | tf_op jit(solution)/shard_map/all_to_all | solution.py:666
  92.1 7.4 %collective-permute-start = (bf16[32,32,128]{2,1,0:T(8,128)(2,1)S(1)}, bf16[32,32,128]{2,1,0:T(8,128)(2,1)S(1)}, u32[]{:S(2)}, u32[]{:S(2)}) collective-permute-start(bf16[32,32,128]{2,1,0:T(8,128)(2,1)S(1)} %combine.1.refs_0_), channel_id=1, source_target_pairs={{0,2},{1,3},{2,0},{3,1},{4,6},{5,7},{6,4},{7,5},{8,10},{9,11},{10,... | collective-permute-start | bytes 786440 | tf_op jit(solution)/shard_map/ppermute | solution.py:679
  93.4 7.6 %collective-permute-start.1 = (bf16[32,32,128]{2,1,0:T(8,128)(2,1)S(1)}, bf16[32,32,128]{2,1,0:T(8,128)(2,1)S(1)}, u32[]{:S(2)}, u32[]{:S(2)}) collective-permute-start(bf16[32,32,128]{2,1,0:T(8,128)(2,1)S(1)} %combine.1.refs_0_), channel_id=1, source_target_pairs={{0,1},{1,0},{2,3},{3,2},{4,5},{5,4},{6,7},{7,6},{8,9},{9,8},{10,11... | collective-permute-start | bytes 786440 | tf_op jit(solution)/shard_map/ppermute | solution.py:679
  99.5 2.5 %collective-permute-start.2 = (bf16[32,32,128]{2,1,0:T(8,128)(2,1)S(1)}, bf16[32,32,128]{2,1,0:T(8,128)(2,1)S(1)}, u32[]{:S(2)}, u32[]{:S(2)}) collective-permute-start(bf16[32,32,128]{2,1,0:T(8,128)(2,1)S(1)} %collective-permute-done.refs_1_), channel_id=1, source_target_pairs={{0,1},{1,0},{2,3},{3,2},{4,5},{5,4},{6,7},{7,6},{8,9},{9,8},{10,11... | collective-permute-start | bytes 786440 | tf_op jit(solution)/shard_map/ppermute | solution.py:679
